TPU v7x, 1024 devices: a whole 4x8x16 slice. The times are simulated.
1024 devices in a mesh: expert: 64 (over x, y, core), dp: 16 (over z).
Axes of the slice: x: 4, y: 8, z: 16, core: 2. Of those that a mesh axis runs over, the one named last changes fastest.
Arguments:
- x_t: bfloat16 [4096, 16384], P('expert', 'dp'), may hold values from -16 to 16
- down_proj: bfloat16 [4096, 1024], P('expert'), may hold values from -0.09375 to 0.09375
- w_gate: bfloat16 [64, 1024, 1024], P('expert'), may hold values from -0.1875 to 0.1875
- w_value: bfloat16 [64, 1024, 1024], P('expert'), may hold values from -0.1875 to 0.1875
- w_out: bfloat16 [64, 1024, 1024], P('expert'), may hold values from -0.1875 to 0.1875
- routes: int32 [16384, 4], P(('dp', 'expert')), may hold values from 0 to 63, all different within a row; in each aligned block of 16 rows (0 to 15, 16 to 31, ...) at most 2 rows name the same one
- gate_fix: int32 [16384, 4], P(('dp', 'expert')), may hold values from 6554 to 65535
- cotangent: bfloat16 [16384, 1024], P(('dp', 'expert')), may hold values from -6 to 6
Outputs:
- combined: bfloat16 [16384, 1024], P(('dp', 'expert'))
- grad_x: bfloat16 [4096, 16384], P('expert', 'dp')
- grad_down: float32 [4096, 1024], P('expert')
Inputs may be any that keep to these rules, and one draw needn't show every extreme that they name: `routes`: each row names 4 different experts. Among the 16 rows of one device (aligned blocks of 16 rows) no expert is named by more than 2 rows, a bound that some block reaches. `gate_fix`: A gate weight is this integer divided by 65536.
All inputs are finite; a program needn't handle non-finite values.
Results may differ from a plain program's by a relative error of at most 0.023.
Values may be sent and summed in bfloat16 or wider, within the bound.
No kernel may reach another device: no remote copies, remote signals or barrier semaphores. Data moves between devices by JAX's collectives and lax.ppermute only.
A program may use at most 32 MiB of HBM per device.

v0:
```python
import math

import jax
import jax.numpy as jnp
from jax import lax
from jax.sharding import PartitionSpec as P

fixed_unit = 65536.0


def contract_first(left, right):
    return lax.dot_general(
        left, right, (((0,), (0,)), ((), ())), preferred_element_type=jnp.float32
    )


def on_device(x_t, down_proj, w_gate, w_value, w_out, routes, gate_fix, cotangent):
    groups = lax.axis_size("expert")
    latent_width = down_proj.shape[1]
    row_count = x_t.shape[1]
    tok_dev = row_count // groups
    route_count = routes.shape[1]
    capacity = max(2, 8 * tok_dev // groups)
    total_tokens = row_count * lax.axis_size("dp")
    flat_routes = routes.reshape(-1)
    chosen = (flat_routes[:, None] == jnp.arange(groups, dtype=jnp.int32)[None, :]).astype(
        jnp.int32
    )
    before = jnp.cumsum(chosen, axis=0) - chosen
    slot_index = jnp.sum(before * chosen, axis=1)
    target = flat_routes * capacity + slot_index
    placing = (jnp.arange(groups * capacity, dtype=jnp.int32)[:, None] == target[None, :]).astype(
        jnp.bfloat16
    )
    gate_values = gate_fix.astype(jnp.float32) / fixed_unit
    grad_rows = (gate_values[:, :, None] * cotangent.astype(jnp.float32)[:, None, :]).astype(
        jnp.bfloat16
    )
    grad_rows = grad_rows.reshape(tok_dev * route_count, latent_width)
    send_grads = jnp.dot(placing, grad_rows, preferred_element_type=jnp.float32).astype(
        jnp.bfloat16
    )
    send_grads = send_grads.reshape(groups, capacity, latent_width)
    columns = x_t
    latent = lax.psum_scatter(
        contract_first(columns, down_proj), "expert", scatter_dimension=0, tiled=True
    ).astype(jnp.bfloat16)
    latent_copies = jnp.repeat(latent, route_count, axis=0)
    send_rows = jnp.dot(placing, latent_copies, preferred_element_type=jnp.float32).astype(
        jnp.bfloat16
    )
    send_rows = send_rows.reshape(groups, capacity, latent_width)
    gate_matrix = w_gate[0]
    value_matrix = w_value[0]
    out_matrix = w_out[0]
    slot_rows = lax.all_to_all(send_rows, "expert", split_axis=0, concat_axis=0, tiled=True)
    slot_grads = lax.all_to_all(send_grads, "expert", split_axis=0, concat_axis=0, tiled=True)
    shape_kept = slot_rows.shape
    flat_rows = slot_rows.reshape(-1, latent_width)
    flat_grads = slot_grads.reshape(-1, latent_width)
    pre_gate = jnp.dot(flat_rows, gate_matrix, preferred_element_type=jnp.float32)
    pre_value = jnp.dot(flat_rows, value_matrix, preferred_element_type=jnp.float32)
    sigmoid_gate = jax.nn.sigmoid(pre_gate)
    activated = pre_gate * sigmoid_gate
    hidden = (activated * pre_value).astype(jnp.bfloat16)
    expert_out = jnp.dot(hidden, out_matrix, preferred_element_type=jnp.float32).astype(
        jnp.bfloat16
    )
    hidden_grad = lax.dot_general(
        flat_grads, out_matrix, (((1,), (1,)), ((), ())), preferred_element_type=jnp.float32
    )
    gate_grad = (
        hidden_grad * pre_value * sigmoid_gate * (1.0 + pre_gate * (1.0 - sigmoid_gate))
    ).astype(jnp.bfloat16)
    value_grad = (hidden_grad * activated).astype(jnp.bfloat16)
    row_grad = lax.dot_general(
        gate_grad, gate_matrix, (((1,), (1,)), ((), ())), preferred_element_type=jnp.float32
    )
    row_grad = row_grad + lax.dot_general(
        value_grad, value_matrix, (((1,), (1,)), ((), ())), preferred_element_type=jnp.float32
    )
    expert_outs = expert_out.reshape(shape_kept)
    expert_grads = row_grad.astype(jnp.bfloat16).reshape(shape_kept)
    back_outs, back_grads = (
        lax.all_to_all(expert_outs, "expert", split_axis=0, concat_axis=0, tiled=True),
        lax.all_to_all(expert_grads, "expert", split_axis=0, concat_axis=0, tiled=True),
    )
    route_outs = contract_first(placing, back_outs.reshape(groups * capacity, latent_width))
    route_grads = contract_first(placing, back_grads.reshape(groups * capacity, latent_width))
    combined = jnp.sum(
        gate_values[:, :, None] * route_outs.reshape(tok_dev, route_count, latent_width), axis=1
    )
    combined = combined.astype(jnp.bfloat16)
    latent_grad = jnp.sum(route_grads.reshape(tok_dev, route_count, latent_width), axis=1).astype(
        jnp.bfloat16
    )
    shard_piece = lax.all_gather(latent_grad, "expert", axis=0, tiled=True)
    columns = lax.dot_general(
        down_proj, shard_piece, (((1,), (1,)), ((), ())), preferred_element_type=jnp.float32
    )
    input_grad = columns
    weight_grad = jnp.dot(x_t, shard_piece, preferred_element_type=jnp.float32)
    input_grad, weight_grad = (input_grad, weight_grad)
    grad_x = input_grad.astype(jnp.bfloat16)
    grad_down = lax.psum(
        (weight_grad * (1.0 / math.sqrt(total_tokens))).astype(jnp.bfloat16), "dp"
    ).astype(jnp.float32)
    return (combined, grad_x, grad_down)


def solution(mesh):
    placed = (
        P("expert", "dp"),
        P("expert", None),
        P("expert", None, None),
        P("expert", None, None),
        P("expert", None, None),
        P(("dp", "expert"), None),
        P(("dp", "expert"), None),
        P(("dp", "expert"), None),
    )
    return jax.shard_map(
        on_device,
        mesh=mesh,
        in_specs=placed,
        out_specs=(P(("dp", "expert"), None), P("expert", "dp"), P("expert", None)),
        check_vma=False,
    )
```

profile of v0, /device:TPU:6, one launch (start us, length us, event | category | flops | bytes accessed | tf_op | source)
XLA Modules:
  0.0 476.9 jit_solution(13895176092846491573)
XLA Ops:
  7.2 0.0 reduce-scatter.2.cloned.1.call-start
  7.2 3.8 fusion.38
  11.0 0.0 reduce-scatter.2.cloned.1.call-update
  11.0 0.7 copy-done.6
  11.7 0.1 copy.13
  11.8 0.1 reshape.90
  11.9 0.1 mul.77
  12.0 0.1 copy.15
  12.1 0.1 mul.74
  12.2 0.1 fusion.32
  12.3 0.1 reduce_window_sum.11
  12.4 0.2 select_reduce_fusion
  12.6 0.3 convolution_convert_fusion
  12.9 0.8 reshape.96
  13.7 17.5 %all-to-all-start.2 = ((bf16[64,2,1024]{2,1,0:T(2,128)(2,1)}), bf16[64,2,1024]{2,1,0:T(2,128)(2,1)S(1)}, u32[]{:S(2)}, u32[]{:S(2)}) async-start(bf16[64,2,1024]{2,1,0:T(2,128)(2,1)} %reshape.96), calls=%async_computation.3 | async-start | bytes 524288 | tf_op jit(solution)/shard_map/all_to_all | solution.py:57
  31.2 158.1 %reduce-scatter.2.cloned.1.call-done = f32[16,1024]{1,0:T(8,128)} async-done(((f32[1024,1024]{1,0:T(8,128)}), f32[16,1024]{1,0:T(8,128)}) %reduce-scatter.2.cloned.1.call-update) | async-done | bytes 65552 | tf_op jit(solution)/shard_map/reduce_scatter | solution.py:45
  189.2 0.8 convert_element_type.61
  190.1 0.2 convolution_convert_fusion.1
  190.3 0.8 reshape.92
  191.1 8.6 %all-to-all-start = ((bf16[64,2,1024]{2,1,0:T(2,128)(2,1)}), bf16[64,2,1024]{2,1,0:T(2,128)(2,1)S(1)}, u32[]{:S(2)}, u32[]{:S(2)}) async-start(bf16[64,2,1024]{2,1,0:T(2,128)(2,1)} %reshape.92), calls=%async_computation.1 | async-start | bytes 524288 | tf_op jit(solution)/shard_map/all_to_all | solution.py:56
  199.8 0.1 reshape.97
  199.9 2.4 fusion
  202.3 9.0 %all-to-all-done = bf16[64,2,1024]{2,1,0:T(2,128)(2,1)S(1)} async-done(((bf16[64,2,1024]{2,1,0:T(2,128)(2,1)}), bf16[64,2,1024]{2,1,0:T(2,128)(2,1)S(1)}, u32[]{:S(2)}, u32[]{:S(2)}) %all-to-all-start) | async-done | bytes 262176 | tf_op jit(solution)/shard_map/all_to_all | solution.py:56
  211.3 0.1 reshape.93
  211.4 0.4 fusion.6
  211.9 1.1 copy-done.1
  213.0 0.4 fusion.10
  213.5 0.8 fusion.4
  214.3 0.9 fusion.18
  215.2 0.8 reshape.98
  216.0 6.5 %all-to-all-start.3 = ((bf16[64,2,1024]{2,1,0:T(2,128)(2,1)}), bf16[64,2,1024]{2,1,0:T(2,128)(2,1)S(1)}, u32[]{:S(2)}, u32[]{:S(2)}) async-start(bf16[64,2,1024]{2,1,0:T(2,128)(2,1)} %reshape.98), calls=%async_computation.4 | async-start | bytes 524288 | tf_op jit(solution)/shard_map/all_to_all | solution.py:86
  222.5 0.0 all-gather.2.cloned.1.call-start
  222.5 0.1 iota_compare_fusion.4
  222.6 11.4 %all-to-all-done.3 = bf16[64,2,1024]{2,1,0:T(2,128)(2,1)S(1)} async-done(((bf16[64,2,1024]{2,1,0:T(2,128)(2,1)}), bf16[64,2,1024]{2,1,0:T(2,128)(2,1)S(1)}, u32[]{:S(2)}, u32[]{:S(2)}) %all-to-all-start.3) | async-done | bytes 262176 | tf_op jit(solution)/shard_map/all_to_all | solution.py:86
  234.1 0.1 reshape.101
  234.2 0.8 convolution_reduce_fusion
  235.0 0.0 all-gather.2.cloned.1.call-update
  235.0 0.0 all-reduce.2.cloned.1.call-start
  235.1 2.3 fusion.15
  237.3 0.1 reshape.94
  237.4 17.8 %all_to_all.20 = bf16[64,2,1024]{2,1,0:T(2,128)(2,1)S(1)} all-to-all(bf16[64,2,1024]{2,1,0:T(2,128)(2,1)S(1)} %reshape.94), channel_id=1, replica_groups=mesh['expert'=64,'dp'=16] {'expert'}, dimensions={0} | all-to-all | bytes 524288 | tf_op jit(solution)/shard_map/all_to_all | solution.py:85
  255.3 0.1 reshape.100
  255.4 0.8 fusion.22
  256.2 68.8 %all-gather.2.cloned.1.call-done = bf16[1024,1024]{1,0:T(8,128)(2,1)} async-done(((bf16[16,1024]{1,0:T(8,128)(2,1)}), bf16[1024,1024]{1,0:T(8,128)(2,1)}) %all-gather.2.cloned.1.call-update) | async-done | bytes 2097168 | tf_op jit(solution)/shard_map/all_gather | solution.py:97
  325.0 2.7 fusion.23
  327.7 3.0 fusion.24
  330.7 138.0 %all-reduce.2.cloned.1.call-done = bf16[64,1024]{1,0:T(8,128)(2,1)} async-done(((bf16[64,1024]{1,0:T(8,128)(2,1)}), bf16[64,1024]{1,0:T(8,128)(2,1)}) %all-reduce.2.cloned.1.call-update) | async-done | bytes 131088 | tf_op jit(solution)/shard_map/psum | solution.py:105
  468.8 1.6 convert_element_type.77
  (21 shorter events, 0.2 us)
Async XLA Ops:
  7.2 204.3 %copy-start = (bf16[1,1024,1024]{2,1,0:T(8,128)(2,1)S(1)}, bf16[1,1024,1024]{2,1,0:T(8,128)(2,1)}, u32[]{:S(2)}) copy-start(bf16[1,1024,1024]{2,1,0:T(8,128)(2,1)} %param.11) | copy-start | bytes 6291460
  7.2 182.0 %reduce-scatter.2.cloned.1.call-start = ((), (), s32[]{:S(2)}) async-start(), calls=%async_computation.5 | async-start | bytes 4259840 | tf_op jit(solution)/shard_map/reduce_scatter | solution.py:45
  11.0 0.7 copy-start.6
  11.0 0.9 copy-start.5
  11.0 1.0 copy-start.7
  13.7 177.5 %all-to-all-start.2 = ((bf16[64,2,1024]{2,1,0:T(2,128)(2,1)}), bf16[64,2,1024]{2,1,0:T(2,128)(2,1)S(1)}, u32[]{:S(2)}, u32[]{:S(2)}) async-start(bf16[64,2,1024]{2,1,0:T(2,128)(2,1)} %reshape.96), calls=%async_computation.3 | async-start | bytes 524288 | tf_op jit(solution)/shard_map/all_to_all | solution.py:57
  191.1 20.2 %all-to-all-start = ((bf16[64,2,1024]{2,1,0:T(2,128)(2,1)}), bf16[64,2,1024]{2,1,0:T(2,128)(2,1)S(1)}, u32[]{:S(2)}, u32[]{:S(2)}) async-start(bf16[64,2,1024]{2,1,0:T(2,128)(2,1)} %reshape.92), calls=%async_computation.1 | async-start | bytes 524288 | tf_op jit(solution)/shard_map/all_to_all | solution.py:56
  211.4 1.6 copy-start.1
  213.5 0.9 copy-start.4
  216.0 18.0 %all-to-all-start.3 = ((bf16[64,2,1024]{2,1,0:T(2,128)(2,1)}), bf16[64,2,1024]{2,1,0:T(2,128)(2,1)S(1)}, u32[]{:S(2)}, u32[]{:S(2)}) async-start(bf16[64,2,1024]{2,1,0:T(2,128)(2,1)} %reshape.98), calls=%async_computation.4 | async-start | bytes 524288 | tf_op jit(solution)/shard_map/all_to_all | solution.py:86
  222.5 102.5 %all-gather.2.cloned.1.call-start = ((), (), s32[]{:S(2)}) async-start(), calls=%async_computation.6 | async-start | bytes 2129920 | tf_op jit(solution)/shard_map/all_gather | solution.py:97
  235.0 90.0 %copy-start.2 = (bf16[64,1024]{1,0:T(8,128)(2,1)S(1)}, bf16[64,1024]{1,0:T(8,128)(2,1)}, u32[]{:S(2)}) copy-start(bf16[64,1024]{1,0:T(8,128)(2,1)} %param.8) | copy-start | bytes 393220
  235.0 233.8 %all-reduce.2.cloned.1.call-start = ((), (), s32[]{:S(2)}) async-start(), calls=%async_computation.7 | async-start | bytes 262144 | tf_op jit(solution)/shard_map/psum | solution.py:105
  237.3 90.4 %copy-start.3 = (bf16[64,1024]{1,0:T(8,128)(2,1)S(1)}, bf16[64,1024]{1,0:T(8,128)(2,1)}, u32[]{:S(2)}) copy-start(bf16[64,1024]{1,0:T(8,128)(2,1)} %param.9) | copy-start | bytes 393220
Sparse Core Ops, SparseCore 0:
  13.9 175.2 reduce-scatter.1
  235.1 89.8 all-gather.1
  327.9 140.7 all-reduce.1
where the time goes:
time: 478 us; the launch traced here: 477 us
  waiting for transfers between devices  385 us (81%)
  starting transfers between devices  32.7 us (7%)
  matrix products  18.9 us (4%)
  blocking collectives  17.8 us (4%)
  between operations  14 us (3%)
  local copies, waits for them, and re-layouts  5.27 us (1%)
    reduce_scatter x1, waiting for transfers between devices, on_device(): lax.psum_scatter(contract_first(columns, down_proj), 'expert', scatter_di...  158 us
    psum x1, waiting for transfers between devices, on_device(): lax.psum((weight_grad * (1.0 / math.sqrt(total_tokens))).astype(jnp.bfloa...  138 us
    all_gather x1, waiting for transfers between devices, on_device(): shard_piece = lax.all_gather(latent_grad, 'expert', axis=0, tiled=True)  68.8 us
    all_to_all x1, blocking collectives, on_device(): lax.all_to_all(expert_outs, 'expert', split_axis=0, concat_axis=0, tiled=...  17.8 us
    all_to_all x1, starting transfers between devices, on_device(): lax.all_to_all(send_grads, 'expert', split_axis=0, concat_axis=0, tiled=T...  17.5 us
    all_to_all x1, waiting for transfers between devices, on_device(): lax.all_to_all(expert_grads, 'expert', split_axis=0, concat_axis=0, tiled...  11.4 us
  transfers between devices with their start and end apart: 6, of which 5 were waited for; matrix products, arithmetic and copies ran while one was open for 3% of the time, Pallas kernels for 0%

commit v1 on v0

v1 whole, which is shorter than its diff:
```python
import math

import jax
import jax.numpy as jnp
from jax import lax
from jax.sharding import Mesh
from jax.sharding import PartitionSpec as P

f32 = jnp.float32
bf16 = jnp.bfloat16


def swap(blocks, axes):
    return lax.all_to_all(blocks, axes, split_axis=0, concat_axis=0, tiled=True)


def on_device(x_t, down_proj, w_gate, w_value, w_out, routes, gate_fix, cotangent):
    nx, ny, nc = lax.axis_size("x"), lax.axis_size("y"), lax.axis_size("c")
    nz = lax.axis_size("dp")
    groups = nx * ny * nc
    feats, width = down_proj.shape
    tokens = x_t.shape[1]
    tok_dev = tokens // groups
    block = tokens // nx
    top = routes.shape[1]
    capacity = max(2, 8 * tok_dev // groups)
    core = lax.axis_index("c")

    flat_routes = routes.reshape(-1)
    chosen = (flat_routes[:, None] == jnp.arange(groups, dtype=jnp.int32)[None, :]).astype(bf16)
    pairs = tok_dev * top
    earlier = (jnp.arange(pairs)[:, None] > jnp.arange(pairs)[None, :]).astype(bf16)
    before = jnp.dot(earlier, chosen, preferred_element_type=f32)
    slot_index = jnp.sum(before * chosen.astype(f32), axis=1).astype(jnp.int32)
    target = flat_routes * capacity + slot_index

    pieces = jnp.transpose(x_t.reshape(feats, nx, block), (1, 0, 2))
    packed = jnp.concatenate(
        [pieces, jnp.broadcast_to(down_proj[None], (nx, feats, width))], axis=2
    )
    packed = swap(packed, "x").reshape(nx * feats, block + width)
    both = lax.all_gather(packed, "c", axis=0, tiled=True)
    partial = lax.dot_general(
        both[:, :block], both[:, block:], (((0,), (0,)), ((), ())), preferred_element_type=f32
    ).astype(bf16)
    partial = partial.reshape(ny, nc, tok_dev, width)
    partial = lax.dynamic_index_in_dim(partial, core, axis=1, keepdims=False)
    latent = jnp.sum(swap(partial, "y").astype(f32), axis=0).astype(bf16)

    slots = groups * capacity
    hit = jnp.arange(slots, dtype=jnp.int32)[:, None] == target[None, :]
    gate_values = gate_fix.astype(f32) / 65536.0
    slot_gate = jnp.sum(jnp.where(hit, gate_values.reshape(1, -1), 0.0), axis=1)
    placing = jnp.sum(hit.reshape(slots, tok_dev, top).astype(f32), axis=2).astype(bf16)
    send_rows = jnp.dot(placing, latent, preferred_element_type=f32).astype(bf16)
    send_grads = slot_gate[:, None] * jnp.dot(placing, cotangent, preferred_element_type=f32)
    send = jnp.concatenate(
        [
            send_rows.reshape(groups, capacity, width),
            send_grads.astype(bf16).reshape(groups, capacity, width),
        ],
        axis=1,
    )
    got = swap(send, ("x", "y", "c"))
    rows = got[:, :capacity].reshape(slots, width)
    grads = got[:, capacity:].reshape(slots, width)

    gate_matrix, value_matrix, out_matrix = w_gate[0], w_value[0], w_out[0]
    last = (((1,), (1,)), ((), ()))
    pre_gate = jnp.dot(rows, gate_matrix, preferred_element_type=f32)
    pre_value = jnp.dot(rows, value_matrix, preferred_element_type=f32)
    sigmoid_gate = jax.nn.sigmoid(pre_gate)
    activated = pre_gate * sigmoid_gate
    hidden = (activated * pre_value).astype(bf16)
    expert_out = jnp.dot(hidden, out_matrix, preferred_element_type=f32).astype(bf16)
    hidden_grad = lax.dot_general(grads, out_matrix, last, preferred_element_type=f32)
    gate_grad = (
        hidden_grad * pre_value * sigmoid_gate * (1.0 + pre_gate * (1.0 - sigmoid_gate))
    ).astype(bf16)
    value_grad = (hidden_grad * activated).astype(bf16)
    row_grad = lax.dot_general(gate_grad, gate_matrix, last, preferred_element_type=f32)
    row_grad += lax.dot_general(value_grad, value_matrix, last, preferred_element_type=f32)
    reply = jnp.concatenate(
        [
            expert_out.reshape(groups, capacity, width),
            row_grad.astype(bf16).reshape(groups, capacity, width),
        ],
        axis=1,
    )
    back = swap(reply, ("x", "y", "c")).reshape(groups * 2 * capacity, width)

    place = jnp.arange(2 * slots, dtype=jnp.int32)
    low_slot = (place // (2 * capacity)) * capacity + place % capacity
    is_grad = (place // capacity) % 2 == 1
    spread = (low_slot[None, None, :] == target.reshape(tok_dev, top)[:, :, None]).astype(f32)
    high = jnp.sum(spread * (gate_fix // 256).astype(f32)[:, :, None], axis=1)
    low = jnp.sum(spread * (gate_fix % 256).astype(f32)[:, :, None], axis=1)
    one = jnp.sum(spread, axis=1)
    chooser = jnp.concatenate(
        [
            jnp.where(is_grad, 0.0, high * (1.0 / 256.0)),
            jnp.where(is_grad, 0.0, low * (1.0 / 65536.0)),
            jnp.where(is_grad, one, 0.0),
        ],
        axis=0,
    ).astype(bf16)
    summed = jnp.dot(chooser, back, preferred_element_type=f32)
    combined = (summed[:tok_dev] + summed[tok_dev : 2 * tok_dev]).astype(bf16)
    latent_grad = summed[2 * tok_dev :].astype(bf16)

    by_y = swap(jnp.broadcast_to(latent_grad[None], (ny, tok_dev, width)), "y")
    by_core = lax.all_gather(by_y, "c", axis=0, tiled=False)
    block_grad = jnp.transpose(by_core, (1, 0, 2, 3)).reshape(block, width)

    own_x, own_proj = packed[:, :block], packed[:, block:]
    scale = 1.0 / math.sqrt(tokens * nz)
    weight_part = jnp.dot(own_x, block_grad, preferred_element_type=f32) * scale
    input_part = lax.dot_general(own_proj, block_grad, last, preferred_element_type=f32)
    packed_back = jnp.concatenate([input_part.astype(bf16), weight_part.astype(bf16)], axis=1)
    packed_back = swap(packed_back.reshape(nx, feats, block + width), "x")
    grad_x = jnp.transpose(packed_back[:, :, :block], (1, 0, 2)).reshape(feats, tokens)
    weight_sum = jnp.sum(packed_back[:, :, block:].astype(f32), axis=0).astype(bf16)

    own_rows = swap(weight_sum.reshape(nz, feats // nz, width), "dp")
    own_rows = jnp.sum(own_rows.astype(f32), axis=0).astype(bf16)
    grad_down = swap(jnp.broadcast_to(own_rows[None], (nz, feats // nz, width)), "dp")
    grad_down = grad_down.reshape(feats, width).astype(f32)
    return (combined, grad_x, grad_down)


def solution(mesh):
    dp = mesh.shape["dp"]
    core = 2
    ny = 8
    nx = mesh.shape["expert"] // (ny * core)
    fine = Mesh(mesh.devices.reshape(nx, ny, core, dp), ("x", "y", "c", "dp"))
    expert = ("x", "y", "c")
    tokens = ("dp", "x", "y", "c")
    placed = (
        P(expert, "dp"),
        P(expert, None),
        P(expert, None, None),
        P(expert, None, None),
        P(expert, None, None),
        P(tokens, None),
        P(tokens, None),
        P(tokens, None),
    )
    return jax.shard_map(
        on_device,
        mesh=fine,
        in_specs=placed,
        out_specs=(P(tokens, None), P(expert, "dp"), P(expert, None)),
        check_vma=False,
    )
```

time: 478 us -> 221 us (0.46)
  waiting for transfers between devices: 385 us -> 60.6 us
  blocking collectives: 17.8 us -> 103 us
  starting transfers between devices: 32.7 us -> 17.2 us
  matrix products: 18.9 us -> 10.4 us
  local copies, waits for them, and re-layouts: 5.27 us -> 10.7 us
    reduce_scatter x1 -> x0, waiting for transfers between devices: 158 us -> none  [on_device(): lax.psum_scatter(contract_first(columns, down_proj), 'expert', scatter_di...]
    psum x1 -> x0, waiting for transfers between devices: 138 us -> none  [on_device(): lax.psum((weight_grad * (1.0 / math.sqrt(total_tokens))).astype(jnp.bfloa...]
    all_to_all x1 -> x5, blocking collectives: 17.8 us -> 101 us  [swap(): return lax.all_to_all(blocks, axes, split_axis=0, concat_axis=0, tiled=True)]
    all_gather x1, waiting for transfers between devices: 68.8 us -> 20.3 us  [on_device(): both = lax.all_gather(packed, 'c', axis=0, tiled=True)]
    all_to_all x3, waiting for transfers between devices: 20.5 us -> 40.3 us  [swap(): return lax.all_to_all(blocks, axes, split_axis=0, concat_axis=0, tiled=True)]
    all_to_all x3, starting transfers between devices: 32.5 us -> 17.1 us  [swap(): return lax.all_to_all(blocks, axes, split_axis=0, concat_axis=0, tiled=True)]
    dot_general x13, matrix products: 18.9 us -> 10.4 us  [the longest x1 2.04 us: on_device(): pre_gate = jnp.dot(rows, gate_matrix, preferred_element_type=f32)]
  transfers between devices with their start and end apart: 6 -> 4, of which waited for: 5 -> 4; matrix products, arithmetic and copies ran while one was open for 3% -> 1% of each run, Pallas kernels for 0% -> 0%
where the time goes in v1:
time: 221 us; the launch traced here: 219 us
  blocking collectives  103 us (47%)
  waiting for transfers between devices  60.6 us (27%)
  starting transfers between devices  17.2 us (8%)
  between operations  14.4 us (7%)
  local copies, waits for them, and re-layouts  10.7 us (5%)
  matrix products  10.4 us (5%)
  other arithmetic  3.1 us (1%)
    all_to_all x5, blocking collectives, swap(): return lax.all_to_all(blocks, axes, split_axis=0, concat_axis=0, tiled=True)  101 us
    all_to_all x3, waiting for transfers between devices, swap(): return lax.all_to_all(blocks, axes, split_axis=0, concat_axis=0, tiled=True)  40.3 us
    all_gather x1, waiting for transfers between devices, on_device(): both = lax.all_gather(packed, 'c', axis=0, tiled=True)  20.3 us
    all_to_all x3, starting transfers between devices, swap(): return lax.all_to_all(blocks, axes, split_axis=0, concat_axis=0, tiled=True)  17.1 us
  transfers between devices with their start and end apart: 4, of which 4 were waited for; matrix products, arithmetic and copies ran while one was open for 1% of the time, Pallas kernels for 0%

profile of v1, /device:TPU:6, one launch (start us, length us, event | category | flops | bytes accessed | tf_op | source)
XLA Modules:
  0.0 219.4 jit_solution(7624620675151448965)
XLA Ops:
  7.2 1.1 reshape.110
  8.4 1.0 broadcast_in_dim.61
  9.4 22.9 %all_to_all.40 = bf16[4,64,1280]{2,1,0:T(8,128)(2,1)} all-to-all(bf16[4,64,1280]{2,1,0:T(8,128)(2,1)S(1)} %pad_maximum_fusion), channel_id=1, replica_groups=mesh['x'=4,'y'=8,'c'=2,'dp'=16] {'x'}, dimensions={0} | all-to-all | bytes 1310720 | tf_op jit(solution)/shard_map/all_to_all | solution.py:14
  32.6 0.2 fusion.23
  33.0 0.1 broadcast_in_dim.62
  33.1 20.3 %all-gather.3.cloned.1.call-done = bf16[512,1280]{1,0:T(8,128)(2,1)} async-done(((bf16[256,1280]{1,0:T(8,128)(2,1)}), bf16[512,1280]{1,0:T(8,128)(2,1)}) %all-gather.3.cloned.1.call-update) | async-done | bytes 1310736 | tf_op jit(solution)/shard_map/all_gather | solution.py:42
  53.4 1.8 convolution_convert_fusion
  55.2 0.7 dynamic-slice_bitcast_fusion
  55.9 6.7 %all-to-all-start.1 = ((bf16[8,16,1024]{2,1,0:T(8,128)(2,1)}), bf16[8,16,1024]{2,1,0:T(8,128)(2,1)S(1)}, u32[]{:S(2)}, u32[]{:S(2)}) async-start(bf16[8,16,1024]{2,1,0:T(8,128)(2,1)} %dynamic-slice_bitcast_fusion), calls=%async_computation.1 | async-start | bytes 524288 | tf_op jit(solution)/shard_map/all_to_all | solution.py:14
  62.7 0.1 select_reduce_fusion
  62.8 0.2 fusion.16
  63.1 0.1 reshape.114
  63.2 11.8 %all-to-all-done.1 = bf16[8,16,1024]{2,1,0:T(8,128)(2,1)S(1)} async-done(((bf16[8,16,1024]{2,1,0:T(8,128)(2,1)}), bf16[8,16,1024]{2,1,0:T(8,128)(2,1)S(1)}, u32[]{:S(2)}, u32[]{:S(2)}) %all-to-all-start.1) | async-done | bytes 262176 | tf_op jit(solution)/shard_map/all_to_all | solution.py:14
  75.0 0.2 convolution_convert_fusion.1
  75.3 0.1 reshape.113
  75.4 0.5 pad_maximum_fusion.2
  76.0 22.1 %all_to_all.41 = bf16[64,4,1024]{2,1,0:T(4,128)(2,1)S(1)} all-to-all(bf16[64,4,1024]{2,1,0:T(4,128)(2,1)S(1)} %pad_maximum_fusion.2), channel_id=1, replica_groups=mesh['x'=4,'y'=8,'c'=2,'dp'=16] {'x','y','c'}, dimensions={0} | all-to-all | bytes 1048576 | tf_op jit(solution)/shard_map/all_to_all | solution.py:14
  98.0 0.4 fusion.60
  98.4 0.1 reshape.115
  98.5 0.1 reshape.117
  98.6 2.0 fusion.10
  100.7 0.5 fusion.6
  101.2 1.1 copy-done.2
  102.3 0.8 fusion
  103.1 0.8 fusion.4
  104.0 0.5 fusion.17
  104.4 1.1 copy-done.3
  105.5 0.8 fusion.20
  106.4 0.1 reshape.118
  106.5 0.1 reshape.116
  106.6 1.3 pad_maximum_fusion.3
  107.9 6.9 %all-to-all-start.3 = ((bf16[64,4,1024]{2,1,0:T(4,128)(2,1)}), bf16[64,4,1024]{2,1,0:T(4,128)(2,1)S(1)}, u32[]{:S(2)}, u32[]{:S(2)}) async-start(bf16[64,4,1024]{2,1,0:T(4,128)(2,1)} %pad_maximum_fusion.3), calls=%async_computation.3 | async-start | bytes 1048576 | tf_op jit(solution)/shard_map/all_to_all | solution.py:14
  115.0 16.5 %all-to-all-done.3 = bf16[64,4,1024]{2,1,0:T(4,128)(2,1)S(1)} async-done(((bf16[64,4,1024]{2,1,0:T(4,128)(2,1)}), bf16[64,4,1024]{2,1,0:T(4,128)(2,1)S(1)}, u32[]{:S(2)}, u32[]{:S(2)}) %all-to-all-start.3) | async-done | bytes 524320 | tf_op jit(solution)/shard_map/all_to_all | solution.py:14
  131.5 0.9 reshape.119
  132.4 1.2 fusion.37
  133.7 15.3 %all_to_all.42 = bf16[8,16,1024]{2,1,0:T(8,128)(2,1)S(1)} all-to-all(bf16[8,16,1024]{2,1,0:T(8,128)(2,1)S(1)} %broadcast_in_dim.65), channel_id=1, replica_groups=mesh['x'=4,'y'=8,'c'=2,'dp'=16] {'y'}, dimensions={0} | all-to-all | bytes 524288 | tf_op jit(solution)/shard_map/all_to_all | solution.py:14
  149.1 2.2 all-gather
  151.3 1.0 convolution_convert_fusion.2
  152.3 0.3 fusion.12
  152.6 1.0 copy.69
  153.7 13.6 %all_to_all.43 = bf16[4,64,1280]{2,1,0:T(8,128)(2,1)S(1)} all-to-all(bf16[4,64,1280]{2,1,0:T(8,128)(2,1)S(1)} %bitcast.48), channel_id=1, replica_groups=mesh['x'=4,'y'=8,'c'=2,'dp'=16] {'x'}, dimensions={0} | all-to-all | bytes 1310720 | tf_op jit(solution)/shard_map/all_to_all | solution.py:14
  167.4 26.8 %all_to_all.44 = bf16[16,4,1024]{2,1,0:T(4,128)(2,1)S(1)} all-to-all(bf16[16,4,1024]{2,1,0:T(4,128)(2,1)S(1)} %reshape.123), channel_id=1, replica_groups=mesh['x'=4,'y'=8,'c'=2,'dp'=16] {'dp'}, dimensions={0} | all-to-all | bytes 262144 | tf_op jit(solution)/shard_map/all_to_all | solution.py:14
  194.3 0.7 broadcast_in_dim.66
  195.0 3.5 %all-to-all-start.7 = ((bf16[16,4,1024]{2,1,0:T(4,128)(2,1)}), bf16[16,4,1024]{2,1,0:T(4,128)(2,1)S(1)}, u32[]{:S(2)}, u32[]{:S(2)}) async-start(bf16[16,4,1024]{2,1,0:T(4,128)(2,1)} %broadcast_in_dim.66), calls=%async_computation.7 | async-start | bytes 262144 | tf_op jit(solution)/shard_map/all_to_all | solution.py:14
  198.5 0.6 fusion.35
  199.1 0.7 copy.73
  199.8 12.0 %all-to-all-done.7 = bf16[16,4,1024]{2,1,0:T(4,128)(2,1)S(1)} async-done(((bf16[16,4,1024]{2,1,0:T(4,128)(2,1)}), bf16[16,4,1024]{2,1,0:T(4,128)(2,1)S(1)}, u32[]{:S(2)}, u32[]{:S(2)}) %all-to-all-start.7) | async-done | bytes 131104 | tf_op jit(solution)/shard_map/all_to_all | solution.py:14
  211.8 0.7 reshape.124
  (41 shorter events, 1.2 us)
Async XLA Ops:
  7.2 93.5 %copy-start = (bf16[1,1024,1024]{2,1,0:T(8,128)(2,1)S(1)}, bf16[1,1024,1024]{2,1,0:T(8,128)(2,1)}, u32[]{:S(2)}) copy-start(bf16[1,1024,1024]{2,1,0:T(8,128)(2,1)} %param.11) | copy-start | bytes 6291460
  7.2 46.2 %all-gather.3.cloned.1.call-start = ((), (), s32[]{:S(2)}) async-start(), calls=%async_computation.8 | async-start | bytes 1966080 | tf_op jit(solution)/shard_map/all_gather | solution.py:42
  8.3 24.0 %copy-start.5 = (s32[16,4]{0,1:T(4,128)S(1)}, s32[16,4]{0,1:T(4,128)}, u32[]{:S(2)}) copy-start(s32[16,4]{0,1:T(4,128)} %param.13) | copy-start | bytes 772
  8.4 24.6 %copy-start.6 = (s32[16,4]{0,1:T(4,128)S(1)}, s32[16,4]{0,1:T(4,128)}, u32[]{:S(2)}) copy-start(s32[16,4]{0,1:T(4,128)} %param.14) | copy-start | bytes 772
  32.4 30.5 %copy-start.4 = (bf16[16,1024]{1,0:T(8,128)(2,1)S(1)}, bf16[16,1024]{1,0:T(8,128)(2,1)}, u32[]{:S(2)}) copy-start(bf16[16,1024]{1,0:T(8,128)(2,1)} %param.15) | copy-start | bytes 98308
  55.9 19.1 %all-to-all-start.1 = ((bf16[8,16,1024]{2,1,0:T(8,128)(2,1)}), bf16[8,16,1024]{2,1,0:T(8,128)(2,1)S(1)}, u32[]{:S(2)}, u32[]{:S(2)}) async-start(bf16[8,16,1024]{2,1,0:T(8,128)(2,1)} %dynamic-slice_bitcast_fusion), calls=%async_computation.1 | async-start | bytes 524288 | tf_op jit(solution)/shard_map/all_to_all | solution.py:14
  100.7 1.6 copy-start.2
  103.9 1.6 copy-start.3
  107.9 23.6 %all-to-all-start.3 = ((bf16[64,4,1024]{2,1,0:T(4,128)(2,1)}), bf16[64,4,1024]{2,1,0:T(4,128)(2,1)S(1)}, u32[]{:S(2)}, u32[]{:S(2)}) async-start(bf16[64,4,1024]{2,1,0:T(4,128)(2,1)} %pad_maximum_fusion.3), calls=%async_computation.3 | async-start | bytes 1048576 | tf_op jit(solution)/shard_map/all_to_all | solution.py:14
  115.0 36.3 %copy-start.1 = (bf16[4,64,1280]{2,1,0:T(8,128)(2,1)S(1)}, bf16[4,64,1280]{2,1,0:T(8,128)(2,1)}, u32[]{:S(2)}) copy-start(bf16[4,64,1280]{2,1,0:T(8,128)(2,1)} %all_to_all.40) | copy-start | bytes 1966084
  195.0 16.8 %all-to-all-start.7 = ((bf16[16,4,1024]{2,1,0:T(4,128)(2,1)}), bf16[16,4,1024]{2,1,0:T(4,128)(2,1)S(1)}, u32[]{:S(2)}, u32[]{:S(2)}) async-start(bf16[16,4,1024]{2,1,0:T(4,128)(2,1)} %broadcast_in_dim.66), calls=%async_computation.7 | async-start | bytes 262144 | tf_op jit(solution)/shard_map/all_to_all | solution.py:14
Sparse Core Ops, SparseCore 0:
  32.5 20.8 all-gather.2

commit v2 on v1

v2 whole, which is shorter than its diff:
```python
import functools
import math

import jax
import jax.numpy as jnp
from jax import lax
from jax.experimental import pallas as pl
from jax.experimental.pallas import tpu as pltpu
from jax.sharding import Mesh
from jax.sharding import PartitionSpec as P

f32 = jnp.float32
bf16 = jnp.bfloat16
MiB = 1 << 20
last = (((1,), (1,)), ((), ()))
first = (((0,), (0,)), ((), ()))


def swap(blocks, axes):
    return lax.all_to_all(blocks, axes, split_axis=0, concat_axis=0, tiled=True)


def local(body, outs, *args, specs=None, limit=8, **static):
    vmem = pl.BlockSpec(memory_space=pltpu.VMEM)
    return pl.pallas_call(
        functools.partial(body, **static) if static else body,
        out_shape=outs,
        in_specs=[vmem] * len(args) if specs is None else specs,
        out_specs=jax.tree.map(lambda _: vmem, outs),
        compiler_params=pltpu.CompilerParams(vmem_limit_bytes=limit * MiB),
    )(*args)


def shape(*dims, dtype=bf16):
    return jax.ShapeDtypeStruct(dims, dtype)


def pack_body(x_ref, proj_ref, out_ref):
    pieces, _, wide = out_ref.shape
    block = wide - proj_ref.shape[1]
    for j in range(pieces):
        out_ref[j, :, :block] = x_ref[:, j * block : (j + 1) * block]
        out_ref[j, :, block:] = proj_ref[...]


def project_body(core_ref, own_ref, other_ref, out_ref):
    ny, rows, width = out_ref.shape
    block = own_ref.shape[1] - width
    part = lax.dot_general(
        own_ref[:, :block], own_ref[:, block:], first, preferred_element_type=f32
    )
    part += lax.dot_general(
        other_ref[:, :block], other_ref[:, block:], first, preferred_element_type=f32
    )
    part = part.reshape(ny, 2, rows, width)
    mine = jnp.where(core_ref[0] == 0, part[:, 0], part[:, 1])
    out_ref[...] = mine.astype(bf16)


def dispatch_body(parts_ref, cot_ref, place_ref, out_ref):
    half = out_ref.shape[1]
    latent = jnp.sum(parts_ref[...].astype(f32), axis=0).astype(bf16)
    cot = cot_ref[...]
    table = jnp.concatenate([latent[:, :half], latent[:, half:], cot[:, :half], cot[:, half:]], 0)
    place = place_ref[...]
    chosen = jnp.where(place != 0.0, 1.0, 0.0).astype(bf16)
    scale = jnp.sum(place, axis=1, keepdims=True)
    rows = jnp.dot(chosen, table, preferred_element_type=f32)
    out_ref[...] = (rows * scale).astype(bf16)


def expert_body(got_ref, gate_ref, value_ref, outw_ref, reply_ref):
    total, half = got_ref.shape
    chunk = 256
    devices = chunk // 8
    to = lax.broadcasted_iota(jnp.int32, (chunk, chunk), 0)
    source = lax.broadcasted_iota(jnp.int32, (chunk, chunk), 1)
    order = jnp.where((to % devices) * 8 + to // devices == source, 1.0, 0.0).astype(bf16)
    sorted_rows = [
        jnp.dot(order, got_ref[c * chunk : (c + 1) * chunk, :], preferred_element_type=f32).astype(
            bf16
        )
        for c in range(total // chunk)
    ]

    def matrix(kind):
        halves = []
        for h in range(2):
            pieces = []
            for piece in sorted_rows:
                for s in range(2):
                    r = (kind * 2 + s) * 2 + h
                    pieces.append(piece[r * devices : (r + 1) * devices])
            halves.append(jnp.concatenate(pieces, axis=0))
        return jnp.concatenate(halves, axis=1)

    rows, grads = matrix(0), matrix(1)
    pre_gate = jnp.dot(rows, gate_ref[0], preferred_element_type=f32)
    pre_value = jnp.dot(rows, value_ref[0], preferred_element_type=f32)
    hidden_grad = lax.dot_general(grads, outw_ref[0], last, preferred_element_type=f32)
    sigmoid_gate = jax.nn.sigmoid(pre_gate)
    activated = pre_gate * sigmoid_gate
    hidden = (activated * pre_value).astype(bf16)
    gate_grad = (
        hidden_grad * pre_value * sigmoid_gate * (1.0 + pre_gate * (1.0 - sigmoid_gate))
    ).astype(bf16)
    value_grad = (hidden_grad * activated).astype(bf16)
    expert_out = jnp.dot(hidden, outw_ref[0], preferred_element_type=f32).astype(bf16)
    row_grad = lax.dot_general(gate_grad, gate_ref[0], last, preferred_element_type=f32)
    row_grad += lax.dot_general(value_grad, value_ref[0], last, preferred_element_type=f32)
    row_grad = row_grad.astype(bf16)
    for c in range(total // chunk):
        pieces = []
        for kind in (expert_out, row_grad):
            for s in range(2):
                at = (c * 2 + s) * devices
                for h in range(2):
                    pieces.append(kind[at : at + devices, h * half : (h + 1) * half])
        stacked = jnp.concatenate(pieces, axis=0)
        reply_ref[c * chunk : (c + 1) * chunk, :] = lax.dot_general(
            order, stacked, first, preferred_element_type=f32
        ).astype(bf16)


def combine_body(back_ref, chooser_ref, combined_ref, spread_ref):
    copies, rows, width = spread_ref.shape
    half = width // 2
    summed = jnp.dot(chooser_ref[...], back_ref[...], preferred_element_type=f32)
    for h in range(2):
        lanes = slice(h * half, (h + 1) * half)
        at = 3 * rows * h
        high, low = summed[at : at + rows], summed[at + rows : at + 2 * rows]
        combined_ref[:, lanes] = (high + low).astype(bf16)
        grad = summed[at + 2 * rows : at + 3 * rows].astype(bf16)
        for j in range(copies):
            spread_ref[j, :, lanes] = grad


def backward_body(grad_ref, packed_ref, out_ref, *, scale):
    cores, ny, rows, width = grad_ref.shape
    block = cores * ny * rows
    grads = jnp.concatenate([grad_ref[c, y] for y in range(ny) for c in range(cores)], axis=0)
    out_ref[:, :block] = lax.dot_general(
        packed_ref[:, block:], grads, last, preferred_element_type=f32
    ).astype(bf16)
    weight = jnp.dot(packed_ref[:, :block], grads, preferred_element_type=f32)
    out_ref[:, block:] = (weight * scale).astype(bf16)


def gather_body(parts_ref, grad_x_ref, weight_ref):
    nx, feats, wide = parts_ref.shape
    block = grad_x_ref.shape[1] // nx
    tiles, tall, half = weight_ref.shape
    for j in range(nx):
        grad_x_ref[:, j * block : (j + 1) * block] = parts_ref[j, :, :block]
    total = jnp.sum(parts_ref[:, :, block:].astype(f32), axis=0).astype(bf16)
    for i in range(tiles):
        a, b = i // 2, i % 2
        weight_ref[i] = total[a * tall : (a + 1) * tall, b * half : (b + 1) * half]


def sum_body(parts_ref, out_ref):
    total = jnp.sum(parts_ref[...].astype(f32), axis=0).astype(bf16)
    out_ref[...] = jnp.broadcast_to(total[None], out_ref.shape)


def finish_body(tiles_ref, out_ref):
    tiles, tall, half = tiles_ref.shape
    for i in range(tiles):
        a, b = i // 2, i % 2
        out_ref[a * tall : (a + 1) * tall, b * half : (b + 1) * half] = tiles_ref[i].astype(f32)


def on_device(x_t, down_proj, w_gate, w_value, w_out, routes, gate_fix, cotangent):
    nx, ny, nc = lax.axis_size("x"), lax.axis_size("y"), lax.axis_size("c")
    nz = lax.axis_size("dp")
    groups = nx * ny * nc
    feats, width = down_proj.shape
    half = width // 2
    tokens = x_t.shape[1]
    tok_dev = tokens // groups
    block = tokens // nx
    top = routes.shape[1]
    pairs = tok_dev * top
    core = lax.axis_index("c").astype(jnp.int32).reshape(1)
    spec = pl.BlockSpec(memory_space=pltpu.VMEM)

    packed = local(pack_body, shape(nx, feats, block + width), x_t, down_proj)
    packed = swap(packed, "x").reshape(nx * feats, block + width)
    other = lax.ppermute(packed, "c", [(0, 1), (1, 0)])
    partial = local(
        project_body,
        shape(ny, tok_dev, width),
        core,
        packed,
        other,
        specs=[pl.BlockSpec(memory_space=pltpu.SMEM), spec, spec],
    )
    parts = swap(partial, "y")

    flat = routes.reshape(-1)
    chosen = (flat[:, None] == jnp.arange(groups, dtype=jnp.int32)[None, :]).astype(bf16)
    earlier = (jnp.arange(pairs)[:, None] > jnp.arange(pairs)[None, :]).astype(bf16)
    before = jnp.dot(earlier, chosen, preferred_element_type=f32)
    slot_index = jnp.sum(before * chosen.astype(f32), axis=1).astype(jnp.int32)
    target = (flat * 2 + slot_index).reshape(tok_dev, top)

    place = jnp.arange(groups * 8, dtype=jnp.int32)
    slot, kind, part = place // 8 * 2 + place % 4 // 2, place % 8 // 4, place % 2
    hit = slot[:, None, None] == target[None]
    gate_values = gate_fix.astype(f32) / 65536.0
    held = jnp.sum(jnp.where(hit, 1.0, 0.0), axis=2)
    gated = jnp.sum(jnp.where(hit, gate_values[None], 0.0), axis=2)
    where = jnp.concatenate(
        [
            jnp.where((kind == q // 2) & (part == q % 2), 1.0, 0.0)[:, None]
            * (held if q < 2 else gated)
            for q in range(4)
        ],
        axis=1,
    )
    spread = jnp.where(target[:, :, None] == slot[None, None, :], 1.0, 0.0)
    high = jnp.sum(spread * (gate_fix // 256).astype(f32)[:, :, None], axis=1) * (1.0 / 256.0)
    low = jnp.sum(spread * (gate_fix % 256).astype(f32)[:, :, None], axis=1) * (1.0 / 65536.0)
    one = jnp.sum(spread, axis=1)
    chooser = jnp.concatenate(
        [
            jnp.where(((kind == k) & (part == h))[None, :], value, 0.0)
            for h in range(2)
            for k, value in ((0, high), (0, low), (1, one))
        ],
        axis=0,
    ).astype(bf16)

    send = local(dispatch_body, shape(groups * 8, half), parts, cotangent, where)
    got = swap(send.reshape(groups, 8, half), ("x", "y", "c")).reshape(groups * 8, half)
    reply = local(
        expert_body, shape(groups * 8, half), got, w_gate, w_value, w_out, limit=32
    )
    back = swap(reply.reshape(groups, 8, half), ("x", "y", "c")).reshape(groups * 8, half)
    combined, by_owner = local(
        combine_body, (shape(tok_dev, width), shape(ny, tok_dev, width)), back, chooser
    )

    by_y = swap(by_owner, "y")
    by_core = lax.all_gather(by_y, "c", axis=0, tiled=False)
    packed_back = local(
        backward_body,
        shape(nx * feats, block + width),
        by_core,
        packed,
        scale=1.0 / math.sqrt(tokens * nz),
    )
    packed_back = swap(packed_back.reshape(nx, feats, block + width), "x")
    grad_x, weight_tiles = local(
        gather_body, (shape(feats, tokens), shape(16, feats // 8, half)), packed_back
    )

    tall = 16 // nz * feats // 8
    own = swap(weight_tiles.reshape(nz, tall, half), "dp")
    own = local(sum_body, shape(nz, tall, half), own)
    tiles = swap(own, "dp").reshape(16, feats // 8, half)
    grad_down = local(finish_body, shape(feats, width, dtype=f32), tiles)
    return (combined, grad_x, grad_down)


def solution(mesh):
    dp = mesh.shape["dp"]
    core = 2
    ny = 8
    nx = mesh.shape["expert"] // (ny * core)
    fine = Mesh(mesh.devices.reshape(nx, ny, core, dp), ("x", "y", "c", "dp"))
    expert = ("x", "y", "c")
    tokens = ("dp", "x", "y", "c")
    placed = (
        P(expert, "dp"),
        P(expert, None),
        P(expert, None, None),
        P(expert, None, None),
        P(expert, None, None),
        P(tokens, None),
        P(tokens, None),
        P(tokens, None),
    )
    return jax.shard_map(
        on_device,
        mesh=fine,
        in_specs=placed,
        out_specs=(P(tokens, None), P(expert, "dp"), P(expert, None)),
        check_vma=False,
    )
```

time: 221 us -> 181 us (0.82)
  blocking collectives: 103 us -> 74.1 us
  starting transfers between devices: 17.2 us -> 35.2 us
  between operations: 14.4 us -> 0.88 us
  waiting for transfers between devices: 60.6 us -> 48.7 us
  matrix products: 10.4 us -> 0.16 us
  Pallas kernels: 0 us -> 9.51 us
    all_to_all x5 -> x4, blocking collectives: 101 us -> 71.9 us  [swap(): return lax.all_to_all(blocks, axes, split_axis=0, concat_axis=0, tiled=True)]
    all_gather x1 -> x0, waiting for transfers between devices: 20.3 us -> none  [on_device(): both = lax.all_gather(packed, 'c', axis=0, tiled=True)]
    all_to_all x3 -> x4, starting transfers between devices: 17.1 us -> 33.3 us  [swap(): return lax.all_to_all(blocks, axes, split_axis=0, concat_axis=0, tiled=True)]
    dot_general x12 -> x0, matrix products: 10.3 us -> none  [the longest x1 2.04 us: on_device(): pre_gate = jnp.dot(rows, gate_matrix, preferred_element_type=f32)]
    pallas_call x0 -> x9, Pallas kernels: none -> 9.51 us  [local(): pl.pallas_call(functools.partial(body, **static) if static else body, out...]
    all_to_all x3 -> x4, waiting for transfers between devices: 40.3 us -> 46.8 us  [swap(): return lax.all_to_all(blocks, axes, split_axis=0, concat_axis=0, tiled=True)]
    unnamed x16 -> x19, local copies, waits for them, and re-layouts: 2.35 us -> 5.87 us
    reshape x10 -> x0, local copies, waits for them, and re-layouts: 3.36 us -> none  [the longest x1 1.12 us: on_device(): pieces = jnp.transpose(x_t.reshape(feats, nx, block), (1, 0, 2))]
  transfers between devices with their start and end apart: 4 -> 5, of which waited for: 4 -> 5; matrix products, arithmetic and copies ran while one was open for 1% -> 3% of each run, Pallas kernels for 0% -> 0%
where the time goes in v2:
time: 181 us; the launch traced here: 180 us
  blocking collectives  74.1 us (41%)
  waiting for transfers between devices  48.7 us (27%)
  starting transfers between devices  35.2 us (19%)
  Pallas kernels  9.51 us (5%)
  local copies, waits for them, and re-layouts  9.45 us (5%)
  other arithmetic  1.82 us (1%)
    all_to_all x4, blocking collectives, swap(): return lax.all_to_all(blocks, axes, split_axis=0, concat_axis=0, tiled=True)  71.9 us
    all_to_all x4, waiting for transfers between devices, swap(): return lax.all_to_all(blocks, axes, split_axis=0, concat_axis=0, tiled=True)  46.8 us
    all_to_all x4, starting transfers between devices, swap(): return lax.all_to_all(blocks, axes, split_axis=0, concat_axis=0, tiled=True)  33.3 us
    pallas_call x9, Pallas kernels, local(): pl.pallas_call(functools.partial(body, **static) if static else body, out...  9.51 us
    unnamed x19, local copies, waits for them, and re-layouts  5.87 us
  transfers between devices with their start and end apart: 5, of which 5 were waited for; matrix products, arithmetic and copies ran while one was open for 3% of the time, Pallas kernels for 0%

profile of v2, /device:TPU:6, one launch (start us, length us, event | category | flops | bytes accessed | tf_op | source)
XLA Modules:
  0.0 179.9 jit_solution(1022247289810647163)
XLA Ops:
  0.6 0.0 copy-start.4
  0.6 0.9 copy-done.4
  1.5 0.0 copy-start.5
  1.5 0.9 copy-done.5
  2.4 0.0 copy-start.8
  2.4 0.9 shard_map.103
  3.3 16.6 %all-to-all-start = ((bf16[4,64,1280]{2,1,0:T(8,128)(2,1)}), bf16[4,64,1280]{2,1,0:T(8,128)(2,1)S(1)}, u32[]{:S(2)}, u32[]{:S(2)}) async-start(bf16[4,64,1280]{2,1,0:T(8,128)(2,1)} %shard_map.103), calls=%async_computation | async-start | bytes 1310720 | tf_op jit(solution)/shard_map/all_to_all | solution.py:20
  19.9 0.0 copy-done.7
  19.9 0.1 copy.38
  20.0 0.1 eq.164
  20.1 0.2 fusion
  20.3 0.1 convert_element_type.30
  20.3 0.1 copy.39
  20.5 6.2 %all-to-all-done = bf16[4,64,1280]{2,1,0:T(8,128)(2,1)S(1)} async-done(((bf16[4,64,1280]{2,1,0:T(8,128)(2,1)}), bf16[4,64,1280]{2,1,0:T(8,128)(2,1)S(1)}, u32[]{:S(2)}, u32[]{:S(2)}) %all-to-all-start) | async-done | bytes 655392 | tf_op jit(solution)/shard_map/all_to_all | solution.py:20
  26.6 1.9 %collective-permute-start = (bf16[256,1280]{1,0:T(8,128)(2,1)S(1)}, bf16[256,1280]{1,0:T(8,128)(2,1)S(1)}, u32[]{:S(2)}, u32[]{:S(2)}) collective-permute-start(bf16[256,1280]{1,0:T(8,128)(2,1)S(1)} %bitcast.8), channel_id=1, source_target_pairs={{0,16},{16,0},{1,17},{17,1},{2,18},{18,2},{3,19},{19,3},{4,20},{20... | collective-permute-start | bytes 1966088 | tf_op jit(solution)/shard_map/ppermute | solution.py:190
  28.6 0.0 copy-done.8
  28.6 0.1 fusion.1
  28.7 1.9 %collective-permute-done.other_ref = bf16[256,1280]{1,0:T(8,128)(2,1)S(1)} collective-permute-done((bf16[256,1280]{1,0:T(8,128)(2,1)S(1)}, bf16[256,1280]{1,0:T(8,128)(2,1)S(1)}, u32[]{:S(2)}, u32[]{:S(2)}) %collective-permute-start) | collective-permute-done | bytes 655392 | tf_op jit(solution)/shard_map/ppermute | solution.py:190
  30.6 1.2 shard_map.104
  31.8 3.4 %all-to-all-start.1 = ((bf16[8,16,1024]{2,1,0:T(8,128)(2,1)}), bf16[8,16,1024]{2,1,0:T(8,128)(2,1)S(1)}, u32[]{:S(2)}, u32[]{:S(2)}) async-start(bf16[8,16,1024]{2,1,0:T(8,128)(2,1)} %shard_map.104), calls=%async_computation.1 | async-start | bytes 524288 | tf_op jit(solution)/shard_map/all_to_all | solution.py:20
  35.2 0.8 copy.42
  36.1 0.8 copy.43
  36.9 0.8 copy.41
  37.7 0.8 copy.40
  38.6 1.5 pad_maximum_fusion.place_ref
  40.0 7.5 %all-to-all-done.1.parts_ref = bf16[8,16,1024]{2,1,0:T(8,128)(2,1)S(1)} async-done(((bf16[8,16,1024]{2,1,0:T(8,128)(2,1)}), bf16[8,16,1024]{2,1,0:T(8,128)(2,1)S(1)}, u32[]{:S(2)}, u32[]{:S(2)}) %all-to-all-start.1) | async-done | bytes 262176 | tf_op jit(solution)/shard_map/all_to_all | solution.py:20
  47.6 0.0 copy-done.6
  47.6 0.3 shard_map.105
  47.9 0.0 copy-start.3
  47.9 0.8 copy-done.3
  48.7 6.4 %all-to-all-start.2 = ((bf16[64,8,512]{2,1,0:T(8,128)(2,1)}), bf16[64,8,512]{2,1,0:T(8,128)(2,1)S(1)}, u32[]{:S(2)}, u32[]{:S(2)}) async-start(bf16[64,8,512]{2,1,0:T(8,128)(2,1)} %bitcast.15), calls=%async_computation.2 | async-start | bytes 1048576 | tf_op jit(solution)/shard_map/all_to_all | solution.py:20
  55.2 0.1 select_reduce_fusion
  55.3 16.5 %all-to-all-done.2 = bf16[64,8,512]{2,1,0:T(8,128)(2,1)S(1)} async-done(((bf16[64,8,512]{2,1,0:T(8,128)(2,1)}), bf16[64,8,512]{2,1,0:T(8,128)(2,1)S(1)}, u32[]{:S(2)}, u32[]{:S(2)}) %all-to-all-start.2) | async-done | bytes 524320 | tf_op jit(solution)/shard_map/all_to_all | solution.py:20
  71.8 0.0 copy-done
  71.9 1.6 copy-done.1
  73.4 1.6 copy-done.2
  75.0 4.4 %shard_map.106 = bf16[512,512]{1,0:T(8,128)(2,1)} custom-call(bf16[512,512]{1,0:T(8,128)(2,1)S(1)} %bitcast.12, bf16[1,1024,1024]{2,1,0:T(8,128)(2,1)S(1)} %copy-done, bf16[1,1024,1024]{2,1,0:T(8,128)(2,1)S(1)} %copy-done.1, bf16[1,1024,1024]{2,1,0:T(8,128)(2,1)S(1)} %copy-done.2), custom_call_target="tpu_custom_call" | custom-call | tf_op jit(solution)/shard_map/pallas_call | solution.py:25
  79.5 6.9 %all-to-all-start.3 = ((bf16[64,8,512]{2,1,0:T(8,128)(2,1)}), bf16[64,8,512]{2,1,0:T(8,128)(2,1)S(1)}, u32[]{:S(2)}, u32[]{:S(2)}) async-start(bf16[64,8,512]{2,1,0:T(8,128)(2,1)} %bitcast.4), calls=%async_computation.3 | async-start | bytes 1048576 | tf_op jit(solution)/shard_map/all_to_all | solution.py:20
  86.5 16.6 %all-to-all-done.3 = bf16[64,8,512]{2,1,0:T(8,128)(2,1)S(1)} async-done(((bf16[64,8,512]{2,1,0:T(8,128)(2,1)}), bf16[64,8,512]{2,1,0:T(8,128)(2,1)S(1)}, u32[]{:S(2)}, u32[]{:S(2)}) %all-to-all-start.3) | async-done | bytes 524320 | tf_op jit(solution)/shard_map/all_to_all | solution.py:20
  103.1 0.8 shard_map.107
  103.9 15.3 %all_to_all.40 = bf16[8,16,1024]{2,1,0:T(8,128)(2,1)S(1)} all-to-all(bf16[8,16,1024]{2,1,0:T(8,128)(2,1)S(1)} %get-tuple-element.8), channel_id=1, replica_groups=mesh['x'=4,'y'=8,'c'=2,'dp'=16] {'y'}, dimensions={0} | all-to-all | bytes 524288 | tf_op jit(solution)/shard_map/all_to_all | solution.py:20
  119.2 2.2 %all-gather = bf16[16,16,1024]{2,1,0:T(8,128)(2,1)S(1)} all-gather(bf16[8,16,1024]{2,1,0:T(8,128)(2,1)S(1)} %all_to_all.40), channel_id=2, replica_groups=mesh['x'=4,'y'=8,'c'=2,'dp'=16] {'c'}, dimensions={0}, use_global_device_ids=true | all-gather | bytes 786432 | tf_op jit(solution)/shard_map/all_gather | solution.py:246
  121.4 0.5 shard_map.108
  121.9 13.6 %all_to_all.41.parts_ref = bf16[4,64,1280]{2,1,0:T(8,128)(2,1)S(1)} all-to-all(bf16[4,64,1280]{2,1,0:T(8,128)(2,1)S(1)} %bitcast.11), channel_id=1, replica_groups=mesh['x'=4,'y'=8,'c'=2,'dp'=16] {'x'}, dimensions={0} | all-to-all | bytes 1310720 | tf_op jit(solution)/shard_map/all_to_all | solution.py:20
  135.5 0.7 shard_map.109
  136.1 26.4 %all_to_all.42.parts_ref = bf16[16,8,512]{2,1,0:T(8,128)(2,1)S(1)} all-to-all(bf16[16,8,512]{2,1,0:T(8,128)(2,1)S(1)} %get-tuple-element.10), channel_id=1, replica_groups=mesh['x'=4,'y'=8,'c'=2,'dp'=16] {'dp'}, dimensions={0} | all-to-all | bytes 262144 | tf_op jit(solution)/shard_map/all_to_all | solution.py:20
  162.6 16.6 %all_to_all.43.tiles_ref = bf16[16,8,512]{2,1,0:T(8,128)(2,1)S(1)} all-to-all(bf16[16,8,512]{2,1,0:T(8,128)(2,1)S(1)} %shard_map.110), channel_id=1, replica_groups=mesh['x'=4,'y'=8,'c'=2,'dp'=16] {'dp'}, dimensions={0} | all-to-all | bytes 262144 | tf_op jit(solution)/shard_map/all_to_all | solution.py:20
  179.2 0.7 shard_map.111
  (26 shorter events, 0.2 us)
Async XLA Ops:
  0.6 0.9 copy-start.4
  1.5 0.9 copy-start.5
  2.4 17.5 %copy-start.7 = (s32[16,4]{0,1:T(4,128)S(1)}, s32[16,4]{0,1:T(4,128)}, u32[]{:S(2)}) copy-start(s32[16,4]{0,1:T(4,128)} %param.13) | copy-start | bytes 772
  2.4 26.1 %copy-start.8 = (s32[16,4]{0,1:T(4,128)S(1)}, s32[16,4]{0,1:T(4,128)}, u32[]{:S(2)}) copy-start(s32[16,4]{0,1:T(4,128)} %param.14) | copy-start | bytes 772
  3.3 23.3 %all-to-all-start = ((bf16[4,64,1280]{2,1,0:T(8,128)(2,1)}), bf16[4,64,1280]{2,1,0:T(8,128)(2,1)S(1)}, u32[]{:S(2)}, u32[]{:S(2)}) async-start(bf16[4,64,1280]{2,1,0:T(8,128)(2,1)} %shard_map.103), calls=%async_computation | async-start | bytes 1310720 | tf_op jit(solution)/shard_map/all_to_all | solution.py:20
  26.6 4.0 %collective-permute-start = (bf16[256,1280]{1,0:T(8,128)(2,1)S(1)}, bf16[256,1280]{1,0:T(8,128)(2,1)S(1)}, u32[]{:S(2)}, u32[]{:S(2)}) collective-permute-start(bf16[256,1280]{1,0:T(8,128)(2,1)S(1)} %bitcast.8), channel_id=1, source_target_pairs={{0,16},{16,0},{1,17},{17,1},{2,18},{18,2},{3,19},{19,3},{4,20},{20... | collective-permute-start | bytes 1966088 | tf_op jit(solution)/shard_map/ppermute | solution.py:190
  30.6 17.0 %copy-start.6 = (bf16[16,1024]{1,0:T(8,128)(2,1)S(1)}, bf16[16,1024]{1,0:T(8,128)(2,1)}, u32[]{:S(2)}) copy-start(bf16[16,1024]{1,0:T(8,128)(2,1)} %cot_ref.1) | copy-start | bytes 98308
  31.8 15.8 %all-to-all-start.1 = ((bf16[8,16,1024]{2,1,0:T(8,128)(2,1)}), bf16[8,16,1024]{2,1,0:T(8,128)(2,1)S(1)}, u32[]{:S(2)}, u32[]{:S(2)}) async-start(bf16[8,16,1024]{2,1,0:T(8,128)(2,1)} %shard_map.104), calls=%async_computation.1 | async-start | bytes 524288 | tf_op jit(solution)/shard_map/all_to_all | solution.py:20
  36.9 35.0 %copy-start = (bf16[1,1024,1024]{2,1,0:T(8,128)(2,1)S(1)}, bf16[1,1024,1024]{2,1,0:T(8,128)(2,1)}, u32[]{:S(2)}) copy-start(bf16[1,1024,1024]{2,1,0:T(8,128)(2,1)} %gate_ref.1) | copy-start | bytes 6291460
  47.9 0.8 copy-start.3
  48.7 23.2 %all-to-all-start.2 = ((bf16[64,8,512]{2,1,0:T(8,128)(2,1)}), bf16[64,8,512]{2,1,0:T(8,128)(2,1)S(1)}, u32[]{:S(2)}, u32[]{:S(2)}) async-start(bf16[64,8,512]{2,1,0:T(8,128)(2,1)} %bitcast.15), calls=%async_computation.2 | async-start | bytes 1048576 | tf_op jit(solution)/shard_map/all_to_all | solution.py:20
  71.9 1.6 copy-start.1
  73.4 1.6 copy-start.2
  79.5 23.6 %all-to-all-start.3 = ((bf16[64,8,512]{2,1,0:T(8,128)(2,1)}), bf16[64,8,512]{2,1,0:T(8,128)(2,1)S(1)}, u32[]{:S(2)}, u32[]{:S(2)}) async-start(bf16[64,8,512]{2,1,0:T(8,128)(2,1)} %bitcast.4), calls=%async_computation.3 | async-start | bytes 1048576 | tf_op jit(solution)/shard_map/all_to_all | solution.py:20

commit v3 on v2

--- a/solution.py
+++ b/solution.py
@@ -20,13 +20,19 @@
     return lax.all_to_all(blocks, axes, split_axis=0, concat_axis=0, tiled=True)
 
 
-def local(body, outs, *args, specs=None, limit=8, **static):
-    vmem = pl.BlockSpec(memory_space=pltpu.VMEM)
+vmem = pl.BlockSpec(memory_space=pltpu.VMEM)
+smem = pl.BlockSpec(memory_space=pltpu.SMEM)
+anywhere = pl.BlockSpec(memory_space=pl.ANY)
+hbm = pl.BlockSpec(memory_space=pltpu.HBM)
+
+
+def local(body, outs, *args, specs=None, out_spec=vmem, scratch=(), limit=8, **static):
     return pl.pallas_call(
         functools.partial(body, **static) if static else body,
         out_shape=outs,
         in_specs=[vmem] * len(args) if specs is None else specs,
-        out_specs=jax.tree.map(lambda _: vmem, outs),
+        out_specs=jax.tree.map(lambda _: out_spec, outs),
+        scratch_shapes=list(scratch),
         compiler_params=pltpu.CompilerParams(vmem_limit_bytes=limit * MiB),
     )(*args)
 
@@ -35,29 +41,47 @@
     return jax.ShapeDtypeStruct(dims, dtype)
 
 
-def pack_body(x_ref, proj_ref, out_ref):
+def pack_body(x_ref, proj_ref, out_ref, sems):
     pieces, _, wide = out_ref.shape
     block = wide - proj_ref.shape[1]
+    copies = []
     for j in range(pieces):
-        out_ref[j, :, :block] = x_ref[:, j * block : (j + 1) * block]
-        out_ref[j, :, block:] = proj_ref[...]
-
-
-def project_body(core_ref, own_ref, other_ref, out_ref):
-    ny, rows, width = out_ref.shape
-    block = own_ref.shape[1] - width
+        copies.append(
+            pltpu.make_async_copy(
+                x_ref.at[:, pl.ds(j * block, block)],
+                out_ref.at[j, :, pl.ds(0, block)],
+                sems.at[2 * j],
+            )
+        )
+        copies.append(
+            pltpu.make_async_copy(
+                proj_ref, out_ref.at[j, :, pl.ds(block, wide - block)], sems.at[2 * j + 1]
+            )
+        )
+    for copy in copies:
+        copy.start()
+    for copy in copies:
+        copy.wait()
+
+
+def project_body(core_ref, packed_ref, mine_ref, theirs_ref):
+    ny, rows, width = mine_ref.shape
+    block = packed_ref.shape[1] - width
     part = lax.dot_general(
-        own_ref[:, :block], own_ref[:, block:], first, preferred_element_type=f32
-    )
-    part += lax.dot_general(
-        other_ref[:, :block], other_ref[:, block:], first, preferred_element_type=f32
-    )
-    part = part.reshape(ny, 2, rows, width)
-    mine = jnp.where(core_ref[0] == 0, part[:, 0], part[:, 1])
-    out_ref[...] = mine.astype(bf16)
-
-
-def dispatch_body(parts_ref, cot_ref, place_ref, out_ref):
+        packed_ref[:, :block], packed_ref[:, block:], first, preferred_element_type=f32
+    )
+    part = part.astype(bf16).reshape(ny, 2, rows, width)
+    even = core_ref[0] == 0
+    mine_ref[...] = jnp.where(even, part[:, 0], part[:, 1])
+    theirs_ref[...] = jnp.where(even, part[:, 1], part[:, 0])
+
+
+def add_body(core_ref, mine_ref, sent_ref, out_ref):
+    other = jnp.where(core_ref[0] == 0, sent_ref[1], sent_ref[0])
+    out_ref[...] = (mine_ref[...].astype(f32) + other.astype(f32)).astype(bf16)
+
+
+def dispatch_body(parts_ref, cot_ref, place_ref, _chooser, out_ref):
     half = out_ref.shape[1]
     latent = jnp.sum(parts_ref[...].astype(f32), axis=0).astype(bf16)
     cot = cot_ref[...]
@@ -183,18 +207,27 @@
     top = routes.shape[1]
     pairs = tok_dev * top
     core = lax.axis_index("c").astype(jnp.int32).reshape(1)
-    spec = pl.BlockSpec(memory_space=pltpu.VMEM)
-
-    packed = local(pack_body, shape(nx, feats, block + width), x_t, down_proj)
+
+    packed = local(
+        pack_body,
+        shape(nx, feats, block + width),
+        x_t,
+        down_proj,
+        specs=[hbm, hbm],
+        scratch=[pltpu.SemaphoreType.DMA((2 * nx,))],
+        limit=60,
+    )
     packed = swap(packed, "x").reshape(nx * feats, block + width)
-    other = lax.ppermute(packed, "c", [(0, 1), (1, 0)])
-    partial = local(
+    mine, theirs = local(
         project_body,
-        shape(ny, tok_dev, width),
+        (shape(ny, tok_dev, width), shape(ny, tok_dev, width)),
         core,
         packed,
-        other,
-        specs=[pl.BlockSpec(memory_space=pltpu.SMEM), spec, spec],
+        specs=[smem, vmem],
+    )
+    sent = lax.all_gather(theirs, "c", axis=0, tiled=False)
+    partial = local(
+        add_body, shape(ny, tok_dev, width), core, mine, sent, specs=[smem, vmem, vmem]
     )
     parts = swap(partial, "y")
 
@@ -232,10 +265,24 @@
         axis=0,
     ).astype(bf16)
 
-    send = local(dispatch_body, shape(groups * 8, half), parts, cotangent, where)
+    send = local(
+        dispatch_body,
+        shape(groups * 8, half),
+        parts,
+        cotangent,
+        where,
+        chooser,
+        specs=[vmem, vmem, vmem, anywhere],
+    )
     got = swap(send.reshape(groups, 8, half), ("x", "y", "c")).reshape(groups * 8, half)
     reply = local(
-        expert_body, shape(groups * 8, half), got, w_gate, w_value, w_out, limit=32
+        expert_body,
+        shape(groups * 8, half),
+        got,
+        w_gate,
+        w_value,
+        w_out,
+        limit=24,
     )
     back = swap(reply.reshape(groups, 8, half), ("x", "y", "c")).reshape(groups * 8, half)
     combined, by_owner = local(

time: 181 us -> 176 us (0.972)
  blocking collectives: 74.1 us -> 122 us
  waiting for transfers between devices: 48.7 us -> 17.2 us
  starting transfers between devices: 35.2 us -> 20 us
  local copies, waits for them, and re-layouts: 9.45 us -> 4.04 us
    all_to_all x4 -> x6, blocking collectives: 71.9 us -> 118 us  [swap(): return lax.all_to_all(blocks, axes, split_axis=0, concat_axis=0, tiled=True)]
    all_to_all x4 -> x2, waiting for transfers between devices: 46.8 us -> 17.2 us  [swap(): return lax.all_to_all(blocks, axes, split_axis=0, concat_axis=0, tiled=True)]
    all_to_all x4 -> x2, starting transfers between devices: 33.3 us -> 20 us  [swap(): return lax.all_to_all(blocks, axes, split_axis=0, concat_axis=0, tiled=True)]
    mul x4, local copies, waits for them, and re-layouts: 3.33 us -> 0.5 us  [on_device(): jnp.where((kind == q // 2) & (part == q % 2), 1.0, 0.0)[:, None]]
    unnamed x19 -> x13, local copies, waits for them, and re-layouts: 5.87 us -> 3.28 us
    all_gather x0 -> x1, blocking collectives: none -> 2.18 us  [on_device(): sent = lax.all_gather(theirs, 'c', axis=0, tiled=False)]
    ppermute x1 -> x0, waiting for transfers between devices: 1.92 us -> none  [on_device(): other = lax.ppermute(packed, 'c', [(0, 1), (1, 0)])]
    ppermute x1 -> x0, starting transfers between devices: 1.91 us -> none  [on_device(): other = lax.ppermute(packed, 'c', [(0, 1), (1, 0)])]
  transfers between devices with their start and end apart: 5 -> 2, of which waited for: 5 -> 2; matrix products, arithmetic and copies ran while one was open for 3% -> 1% of each run, Pallas kernels for 0% -> 0%
where the time goes in v3:
time: 176 us; the launch traced here: 175 us
  blocking collectives  122 us (69%)
  starting transfers between devices  20 us (11%)
  waiting for transfers between devices  17.2 us (10%)
  Pallas kernels  9.94 us (6%)
  local copies, waits for them, and re-layouts  4.04 us (2%)
    all_to_all x6, blocking collectives, swap(): return lax.all_to_all(blocks, axes, split_axis=0, concat_axis=0, tiled=True)  118 us
    all_to_all x2, starting transfers between devices, swap(): return lax.all_to_all(blocks, axes, split_axis=0, concat_axis=0, tiled=True)  20 us
    all_to_all x2, waiting for transfers between devices, swap(): return lax.all_to_all(blocks, axes, split_axis=0, concat_axis=0, tiled=True)  17.2 us
    pallas_call x10, Pallas kernels, local(): pl.pallas_call(functools.partial(body, **static) if static else body, out...  9.94 us
  transfers between devices with their start and end apart: 2, of which 2 were waited for; matrix products, arithmetic and copies ran while one was open for 1% of the time, Pallas kernels for 0%

profile of v3, /device:TPU:6, one launch (start us, length us, event | category | flops | bytes accessed | tf_op | source)
XLA Modules:
  0.0 174.9 jit_solution(10136360950323115941)
XLA Ops:
  0.6 0.0 copy-start.5
  0.6 0.0 copy-start.4
  0.7 2.2 %shard_map.103 = bf16[4,64,1280]{2,1,0:T(8,128)(2,1)} custom-call(bf16[64,1024]{1,0:T(8,128)(2,1)} %x_ref.1, bf16[64,1024]{1,0:T(8,128)(2,1)} %proj_ref.1), custom_call_target="tpu_custom_call" | custom-call | tf_op jit(solution)/shard_map/pallas_call | solution.py:30
  2.8 16.6 %all-to-all-start = ((bf16[4,64,1280]{2,1,0:T(8,128)(2,1)}), bf16[4,64,1280]{2,1,0:T(8,128)(2,1)S(1)}, u32[]{:S(2)}, u32[]{:S(2)}) async-start(bf16[4,64,1280]{2,1,0:T(8,128)(2,1)} %shard_map.103), calls=%async_computation | async-start | bytes 1310720 | tf_op jit(solution)/shard_map/all_to_all | solution.py:20
  19.5 0.0 copy-done.5
  19.6 0.0 copy-done.4
  19.6 0.1 copy.38
  19.7 0.1 eq.164
  19.8 0.2 fusion
  19.9 0.1 convert_element_type.30
  20.0 0.1 copy.39
  20.1 0.1 fusion.1
  20.2 0.1 copy.42
  20.4 0.1 copy.43
  20.5 0.1 copy.41
  20.6 0.1 copy.40
  20.8 0.1 select_reduce_fusion
  20.9 0.0 copy-start.3
  20.9 0.3 pad_maximum_fusion.place_ref
  21.2 4.9 %all-to-all-done = bf16[4,64,1280]{2,1,0:T(8,128)(2,1)S(1)} async-done(((bf16[4,64,1280]{2,1,0:T(8,128)(2,1)}), bf16[4,64,1280]{2,1,0:T(8,128)(2,1)S(1)}, u32[]{:S(2)}, u32[]{:S(2)}) %all-to-all-start) | async-done | bytes 655392 | tf_op jit(solution)/shard_map/all_to_all | solution.py:20
  26.1 0.3 shard_map.104
  26.5 2.2 %all-gather = bf16[16,16,1024]{2,1,0:T(8,128)(2,1)S(1)} all-gather(bf16[8,16,1024]{2,1,0:T(8,128)(2,1)S(1)} %get-tuple-element.10), channel_id=2, replica_groups=mesh['x'=4,'y'=8,'c'=2,'dp'=16] {'c'}, dimensions={0}, use_global_device_ids=true | all-gather | bytes 786432 | tf_op jit(solution)/shard_map/all_gather | solution.py:228
  28.7 0.0 copy-start
  28.7 0.8 shard_map.105
  29.4 3.4 %all-to-all-start.1 = ((bf16[8,16,1024]{2,1,0:T(8,128)(2,1)}), bf16[8,16,1024]{2,1,0:T(8,128)(2,1)S(1)}, u32[]{:S(2)}, u32[]{:S(2)}) async-start(bf16[8,16,1024]{2,1,0:T(8,128)(2,1)} %shard_map.105), calls=%async_computation.1 | async-start | bytes 524288 | tf_op jit(solution)/shard_map/all_to_all | solution.py:20
  32.9 12.3 %all-to-all-done.1.parts_ref = bf16[8,16,1024]{2,1,0:T(8,128)(2,1)S(1)} async-done(((bf16[8,16,1024]{2,1,0:T(8,128)(2,1)}), bf16[8,16,1024]{2,1,0:T(8,128)(2,1)S(1)}, u32[]{:S(2)}, u32[]{:S(2)}) %all-to-all-start.1) | async-done | bytes 262176 | tf_op jit(solution)/shard_map/all_to_all | solution.py:20
  45.2 0.0 copy-done.3
  45.2 0.3 shard_map.106
  45.5 22.3 %all_to_all.40 = bf16[64,8,512]{2,1,0:T(8,128)(2,1)S(1)} all-to-all(bf16[64,8,512]{2,1,0:T(8,128)(2,1)S(1)} %bitcast.17), channel_id=1, replica_groups=mesh['x'=4,'y'=8,'c'=2,'dp'=16] {'x','y','c'}, dimensions={0} | all-to-all | bytes 1048576 | tf_op jit(solution)/shard_map/all_to_all | solution.py:20
  67.9 0.0 copy-done
  67.9 0.0 copy-start.1
  67.9 1.6 copy-done.1
  69.5 0.0 copy-start.2
  69.5 1.6 copy-done.2
  71.1 3.6 %shard_map.107 = bf16[512,512]{1,0:T(8,128)(2,1)S(1)} custom-call(bf16[512,512]{1,0:T(8,128)(2,1)S(1)} %bitcast.12, bf16[1,1024,1024]{2,1,0:T(8,128)(2,1)S(1)} %copy-done, bf16[1,1024,1024]{2,1,0:T(8,128)(2,1)S(1)} %copy-done.1, bf16[1,1024,1024]{2,1,0:T(8,128)(2,1)S(1)} %copy-done.2), custom_call_target="tpu_custom_call" | custom-call | tf_op jit(solution)/shard_map/pallas_call | solution.py:30
  74.7 23.4 %all_to_all.41 = bf16[64,8,512]{2,1,0:T(8,128)(2,1)S(1)} all-to-all(bf16[64,8,512]{2,1,0:T(8,128)(2,1)S(1)} %bitcast.13), channel_id=1, replica_groups=mesh['x'=4,'y'=8,'c'=2,'dp'=16] {'x','y','c'}, dimensions={0} | all-to-all | bytes 1048576 | tf_op jit(solution)/shard_map/all_to_all | solution.py:20
  98.1 0.8 shard_map.108
  98.9 15.3 %all_to_all.42 = bf16[8,16,1024]{2,1,0:T(8,128)(2,1)S(1)} all-to-all(bf16[8,16,1024]{2,1,0:T(8,128)(2,1)S(1)} %get-tuple-element.12), channel_id=1, replica_groups=mesh['x'=4,'y'=8,'c'=2,'dp'=16] {'y'}, dimensions={0} | all-to-all | bytes 524288 | tf_op jit(solution)/shard_map/all_to_all | solution.py:20
  114.3 2.2 %all-gather.1 = bf16[16,16,1024]{2,1,0:T(8,128)(2,1)S(1)} all-gather(bf16[8,16,1024]{2,1,0:T(8,128)(2,1)S(1)} %all_to_all.42), channel_id=3, replica_groups=mesh['x'=4,'y'=8,'c'=2,'dp'=16] {'c'}, dimensions={0}, use_global_device_ids=true | all-gather | bytes 786432 | tf_op jit(solution)/shard_map/all_gather | solution.py:293
  116.4 0.5 shard_map.109
  116.9 13.6 %all_to_all.43.parts_ref = bf16[4,64,1280]{2,1,0:T(8,128)(2,1)S(1)} all-to-all(bf16[4,64,1280]{2,1,0:T(8,128)(2,1)S(1)} %bitcast.11), channel_id=1, replica_groups=mesh['x'=4,'y'=8,'c'=2,'dp'=16] {'x'}, dimensions={0} | all-to-all | bytes 1310720 | tf_op jit(solution)/shard_map/all_to_all | solution.py:20
  130.5 0.7 shard_map.110
  131.2 26.4 %all_to_all.44.parts_ref = bf16[16,8,512]{2,1,0:T(8,128)(2,1)S(1)} all-to-all(bf16[16,8,512]{2,1,0:T(8,128)(2,1)S(1)} %get-tuple-element.14), channel_id=1, replica_groups=mesh['x'=4,'y'=8,'c'=2,'dp'=16] {'dp'}, dimensions={0} | all-to-all | bytes 262144 | tf_op jit(solution)/shard_map/all_to_all | solution.py:20
  157.6 16.6 %all_to_all.45.tiles_ref = bf16[16,8,512]{2,1,0:T(8,128)(2,1)S(1)} all-to-all(bf16[16,8,512]{2,1,0:T(8,128)(2,1)S(1)} %shard_map.111), channel_id=1, replica_groups=mesh['x'=4,'y'=8,'c'=2,'dp'=16] {'dp'}, dimensions={0} | all-to-all | bytes 262144 | tf_op jit(solution)/shard_map/all_to_all | solution.py:20
  174.2 0.7 shard_map.112
  (21 shorter events, 0.2 us)
Async XLA Ops:
  0.6 18.9 %copy-start.5 = (s32[16,4]{0,1:T(4,128)S(1)}, s32[16,4]{0,1:T(4,128)}, u32[]{:S(2)}) copy-start(s32[16,4]{0,1:T(4,128)} %param.14) | copy-start | bytes 772
  0.6 18.9 %copy-start.4 = (s32[16,4]{0,1:T(4,128)S(1)}, s32[16,4]{0,1:T(4,128)}, u32[]{:S(2)}) copy-start(s32[16,4]{0,1:T(4,128)} %param.13) | copy-start | bytes 772
  2.8 23.3 %all-to-all-start = ((bf16[4,64,1280]{2,1,0:T(8,128)(2,1)}), bf16[4,64,1280]{2,1,0:T(8,128)(2,1)S(1)}, u32[]{:S(2)}, u32[]{:S(2)}) async-start(bf16[4,64,1280]{2,1,0:T(8,128)(2,1)} %shard_map.103), calls=%async_computation | async-start | bytes 1310720 | tf_op jit(solution)/shard_map/all_to_all | solution.py:20
  20.9 24.3 %copy-start.3 = (bf16[16,1024]{1,0:T(8,128)(2,1)S(1)}, bf16[16,1024]{1,0:T(8,128)(2,1)}, u32[]{:S(2)}) copy-start(bf16[16,1024]{1,0:T(8,128)(2,1)} %cot_ref.1) | copy-start | bytes 98308
  28.7 39.2 %copy-start = (bf16[1,1024,1024]{2,1,0:T(8,128)(2,1)S(1)}, bf16[1,1024,1024]{2,1,0:T(8,128)(2,1)}, u32[]{:S(2)}) copy-start(bf16[1,1024,1024]{2,1,0:T(8,128)(2,1)} %gate_ref.1) | copy-start | bytes 6291460
  29.4 15.8 %all-to-all-start.1 = ((bf16[8,16,1024]{2,1,0:T(8,128)(2,1)}), bf16[8,16,1024]{2,1,0:T(8,128)(2,1)S(1)}, u32[]{:S(2)}, u32[]{:S(2)}) async-start(bf16[8,16,1024]{2,1,0:T(8,128)(2,1)} %shard_map.105), calls=%async_computation.1 | async-start | bytes 524288 | tf_op jit(solution)/shard_map/all_to_all | solution.py:20
  67.9 1.6 copy-start.1
  69.5 1.6 copy-start.2

commit v4 on v3

--- a/solution.py
+++ b/solution.py
@@ -41,27 +41,21 @@
     return jax.ShapeDtypeStruct(dims, dtype)
 
 
-def pack_body(x_ref, proj_ref, out_ref, sems):
+def pack_body(x_hbm, proj_hbm, out_ref, x_ref, proj_ref, sems):
     pieces, _, wide = out_ref.shape
     block = wide - proj_ref.shape[1]
-    copies = []
+    loads = [
+        pltpu.make_async_copy(x_hbm, x_ref, sems.at[0]),
+        pltpu.make_async_copy(proj_hbm, proj_ref, sems.at[1]),
+    ]
+    for load in loads:
+        load.start()
+    loads[0].wait()
     for j in range(pieces):
-        copies.append(
-            pltpu.make_async_copy(
-                x_ref.at[:, pl.ds(j * block, block)],
-                out_ref.at[j, :, pl.ds(0, block)],
-                sems.at[2 * j],
-            )
-        )
-        copies.append(
-            pltpu.make_async_copy(
-                proj_ref, out_ref.at[j, :, pl.ds(block, wide - block)], sems.at[2 * j + 1]
-            )
-        )
-    for copy in copies:
-        copy.start()
-    for copy in copies:
-        copy.wait()
+        out_ref[j, :, :block] = x_ref[:, j * block : (j + 1) * block]
+    loads[1].wait()
+    for j in range(pieces):
+        out_ref[j, :, block:] = proj_ref[...]
 
 
 def project_body(core_ref, packed_ref, mine_ref, theirs_ref):
@@ -93,7 +87,33 @@
     out_ref[...] = (rows * scale).astype(bf16)
 
 
-def expert_body(got_ref, gate_ref, value_ref, outw_ref, reply_ref):
+def expert_body(
+    got_ref, gate_ref, value_hbm, outw_hbm, reply_ref, value_ref, outw_ref, sems
+):
+    loads = []
+    count = sems.shape[1]
+    for i, (source, target) in enumerate(
+        ((value_hbm, value_ref), (outw_hbm, outw_ref))
+    ):
+        tall = source.shape[1] // count
+        loads.append(
+            [
+                pltpu.make_async_copy(
+                    source.at[0, pl.ds(j * tall, tall)],
+                    target.at[0, pl.ds(j * tall, tall)],
+                    sems.at[i, j],
+                )
+                for j in range(count)
+            ]
+        )
+    for group in loads:
+        for load in group:
+            load.start()
+
+    def arrived(i):
+        for load in loads[i]:
+            load.wait()
+
     total, half = got_ref.shape
     chunk = 256
     devices = chunk // 8
@@ -120,7 +140,9 @@
 
     rows, grads = matrix(0), matrix(1)
     pre_gate = jnp.dot(rows, gate_ref[0], preferred_element_type=f32)
+    arrived(0)
     pre_value = jnp.dot(rows, value_ref[0], preferred_element_type=f32)
+    arrived(1)
     hidden_grad = lax.dot_general(grads, outw_ref[0], last, preferred_element_type=f32)
     sigmoid_gate = jax.nn.sigmoid(pre_gate)
     activated = pre_gate * sigmoid_gate
@@ -214,7 +236,11 @@
         x_t,
         down_proj,
         specs=[hbm, hbm],
-        scratch=[pltpu.SemaphoreType.DMA((2 * nx,))],
+        scratch=[
+            pltpu.VMEM(x_t.shape, bf16),
+            pltpu.VMEM(down_proj.shape, bf16),
+            pltpu.SemaphoreType.DMA((2,)),
+        ],
         limit=60,
     )
     packed = swap(packed, "x").reshape(nx * feats, block + width)
@@ -282,7 +308,13 @@
         w_gate,
         w_value,
         w_out,
-        limit=24,
+        specs=[vmem, vmem, hbm, hbm],
+        scratch=[
+            pltpu.VMEM(w_value.shape, bf16),
+            pltpu.VMEM(w_out.shape, bf16),
+            pltpu.SemaphoreType.DMA((2, 4)),
+        ],
+        limit=50,
     )
     back = swap(reply.reshape(groups, 8, half), ("x", "y", "c")).reshape(groups * 8, half)
     combined, by_owner = local(

time: 176 us -> 174 us (0.989)
  local copies, waits for them, and re-layouts: 4.04 us -> 0.86 us
    unnamed x13 -> x9, local copies, waits for them, and re-layouts: 3.28 us -> 0.1 us
where the time goes in v4:
time: 174 us; the launch traced here: 173 us
  blocking collectives  122 us (70%)
  starting transfers between devices  20 us (11%)
  waiting for transfers between devices  17.2 us (10%)
  Pallas kernels  11.1 us (6%)
    all_to_all x6, blocking collectives, swap(): return lax.all_to_all(blocks, axes, split_axis=0, concat_axis=0, tiled=True)  118 us
    all_to_all x2, starting transfers between devices, swap(): return lax.all_to_all(blocks, axes, split_axis=0, concat_axis=0, tiled=True)  20 us
    all_to_all x2, waiting for transfers between devices, swap(): return lax.all_to_all(blocks, axes, split_axis=0, concat_axis=0, tiled=True)  17.2 us
    pallas_call x10, Pallas kernels, local(): pl.pallas_call(functools.partial(body, **static) if static else body, out...  11.1 us
  transfers between devices with their start and end apart: 2, of which 2 were waited for; matrix products, arithmetic and copies ran while one was open for 1% of the time, Pallas kernels for 0%

profile of v4, /device:TPU:6, one launch (start us, length us, event | category | flops | bytes accessed | tf_op | source)
XLA Modules:
  0.0 172.9 jit_solution(11114776074489239262)
XLA Ops:
  0.6 0.0 copy-start.3
  0.6 0.0 copy-start.2
  0.7 1.9 %shard_map.103 = bf16[4,64,1280]{2,1,0:T(8,128)(2,1)} custom-call(bf16[64,1024]{1,0:T(8,128)(2,1)} %x_hbm.1, bf16[64,1024]{1,0:T(8,128)(2,1)} %proj_hbm.1), custom_call_target="tpu_custom_call" | custom-call | tf_op jit(solution)/shard_map/pallas_call | solution.py:30
  2.5 16.6 %all-to-all-start = ((bf16[4,64,1280]{2,1,0:T(8,128)(2,1)}), bf16[4,64,1280]{2,1,0:T(8,128)(2,1)S(1)}, u32[]{:S(2)}, u32[]{:S(2)}) async-start(bf16[4,64,1280]{2,1,0:T(8,128)(2,1)} %shard_map.103), calls=%async_computation | async-start | bytes 1310720 | tf_op jit(solution)/shard_map/all_to_all | solution.py:20
  19.2 0.0 copy-done.3
  19.3 0.0 copy-done.2
  19.3 0.1 copy.38
  19.4 0.1 eq.164
  19.4 0.2 fusion
  19.6 0.1 convert_element_type.30
  19.7 0.1 copy.39
  19.8 0.1 fusion.1
  19.9 0.1 copy.42
  20.1 0.1 copy.43
  20.2 0.1 copy.41
  20.3 0.1 copy.40
  20.5 0.1 select_reduce_fusion
  20.6 0.0 copy-start.1
  20.6 0.3 pad_maximum_fusion.place_ref
  20.9 4.9 %all-to-all-done = bf16[4,64,1280]{2,1,0:T(8,128)(2,1)S(1)} async-done(((bf16[4,64,1280]{2,1,0:T(8,128)(2,1)}), bf16[4,64,1280]{2,1,0:T(8,128)(2,1)S(1)}, u32[]{:S(2)}, u32[]{:S(2)}) %all-to-all-start) | async-done | bytes 655392 | tf_op jit(solution)/shard_map/all_to_all | solution.py:20
  25.8 0.3 shard_map.104
  26.2 2.2 %all-gather = bf16[16,16,1024]{2,1,0:T(8,128)(2,1)S(1)} all-gather(bf16[8,16,1024]{2,1,0:T(8,128)(2,1)S(1)} %get-tuple-element.10), channel_id=2, replica_groups=mesh['x'=4,'y'=8,'c'=2,'dp'=16] {'c'}, dimensions={0}, use_global_device_ids=true | all-gather | bytes 786432 | tf_op jit(solution)/shard_map/all_gather | solution.py:254
  28.3 0.0 copy-start
  28.3 0.8 shard_map.105
  29.1 3.4 %all-to-all-start.1 = ((bf16[8,16,1024]{2,1,0:T(8,128)(2,1)}), bf16[8,16,1024]{2,1,0:T(8,128)(2,1)S(1)}, u32[]{:S(2)}, u32[]{:S(2)}) async-start(bf16[8,16,1024]{2,1,0:T(8,128)(2,1)} %shard_map.105), calls=%async_computation.1 | async-start | bytes 524288 | tf_op jit(solution)/shard_map/all_to_all | solution.py:20
  32.6 12.3 %all-to-all-done.1.parts_ref = bf16[8,16,1024]{2,1,0:T(8,128)(2,1)S(1)} async-done(((bf16[8,16,1024]{2,1,0:T(8,128)(2,1)}), bf16[8,16,1024]{2,1,0:T(8,128)(2,1)S(1)}, u32[]{:S(2)}, u32[]{:S(2)}) %all-to-all-start.1) | async-done | bytes 262176 | tf_op jit(solution)/shard_map/all_to_all | solution.py:20
  44.9 0.0 copy-done.1
  44.9 0.3 shard_map.106
  45.2 22.3 %all_to_all.40 = bf16[64,8,512]{2,1,0:T(8,128)(2,1)S(1)} all-to-all(bf16[64,8,512]{2,1,0:T(8,128)(2,1)S(1)} %bitcast.17), channel_id=1, replica_groups=mesh['x'=4,'y'=8,'c'=2,'dp'=16] {'x','y','c'}, dimensions={0} | all-to-all | bytes 1048576 | tf_op jit(solution)/shard_map/all_to_all | solution.py:20
  67.6 0.0 copy-done
  67.6 5.1 %shard_map.107 = bf16[512,512]{1,0:T(8,128)(2,1)S(1)} custom-call(bf16[512,512]{1,0:T(8,128)(2,1)S(1)} %bitcast.12, bf16[1,1024,1024]{2,1,0:T(8,128)(2,1)S(1)} %copy-done, bf16[1,1024,1024]{2,1,0:T(8,128)(2,1)} %value_hbm.1, bf16[1,1024,1024]{2,1,0:T(8,128)(2,1)} %outw_hbm.1), custom_call_target="tpu_custom_call" | custom-call | tf_op jit(solution)/shard_map/pallas_call | solution.py:30
  72.7 23.4 %all_to_all.41 = bf16[64,8,512]{2,1,0:T(8,128)(2,1)S(1)} all-to-all(bf16[64,8,512]{2,1,0:T(8,128)(2,1)S(1)} %bitcast.13), channel_id=1, replica_groups=mesh['x'=4,'y'=8,'c'=2,'dp'=16] {'x','y','c'}, dimensions={0} | all-to-all | bytes 1048576 | tf_op jit(solution)/shard_map/all_to_all | solution.py:20
  96.1 0.8 shard_map.108
  96.9 15.3 %all_to_all.42 = bf16[8,16,1024]{2,1,0:T(8,128)(2,1)S(1)} all-to-all(bf16[8,16,1024]{2,1,0:T(8,128)(2,1)S(1)} %get-tuple-element.12), channel_id=1, replica_groups=mesh['x'=4,'y'=8,'c'=2,'dp'=16] {'y'}, dimensions={0} | all-to-all | bytes 524288 | tf_op jit(solution)/shard_map/all_to_all | solution.py:20
  112.2 2.2 %all-gather.1 = bf16[16,16,1024]{2,1,0:T(8,128)(2,1)S(1)} all-gather(bf16[8,16,1024]{2,1,0:T(8,128)(2,1)S(1)} %all_to_all.42), channel_id=3, replica_groups=mesh['x'=4,'y'=8,'c'=2,'dp'=16] {'c'}, dimensions={0}, use_global_device_ids=true | all-gather | bytes 786432 | tf_op jit(solution)/shard_map/all_gather | solution.py:325
  114.4 0.5 shard_map.109
  114.9 13.6 %all_to_all.43.parts_ref = bf16[4,64,1280]{2,1,0:T(8,128)(2,1)S(1)} all-to-all(bf16[4,64,1280]{2,1,0:T(8,128)(2,1)S(1)} %bitcast.11), channel_id=1, replica_groups=mesh['x'=4,'y'=8,'c'=2,'dp'=16] {'x'}, dimensions={0} | all-to-all | bytes 1310720 | tf_op jit(solution)/shard_map/all_to_all | solution.py:20
  128.5 0.7 shard_map.110
  129.2 26.4 %all_to_all.44.parts_ref = bf16[16,8,512]{2,1,0:T(8,128)(2,1)S(1)} all-to-all(bf16[16,8,512]{2,1,0:T(8,128)(2,1)S(1)} %get-tuple-element.14), channel_id=1, replica_groups=mesh['x'=4,'y'=8,'c'=2,'dp'=16] {'dp'}, dimensions={0} | all-to-all | bytes 262144 | tf_op jit(solution)/shard_map/all_to_all | solution.py:20
  155.6 16.6 %all_to_all.45.tiles_ref = bf16[16,8,512]{2,1,0:T(8,128)(2,1)S(1)} all-to-all(bf16[16,8,512]{2,1,0:T(8,128)(2,1)S(1)} %shard_map.111), channel_id=1, replica_groups=mesh['x'=4,'y'=8,'c'=2,'dp'=16] {'dp'}, dimensions={0} | all-to-all | bytes 262144 | tf_op jit(solution)/shard_map/all_to_all | solution.py:20
  172.2 0.7 shard_map.112
  (21 shorter events, 0.2 us)
Async XLA Ops:
  0.6 18.6 %copy-start.3 = (s32[16,4]{0,1:T(4,128)S(1)}, s32[16,4]{0,1:T(4,128)}, u32[]{:S(2)}) copy-start(s32[16,4]{0,1:T(4,128)} %param.14) | copy-start | bytes 772
  0.6 18.6 %copy-start.2 = (s32[16,4]{0,1:T(4,128)S(1)}, s32[16,4]{0,1:T(4,128)}, u32[]{:S(2)}) copy-start(s32[16,4]{0,1:T(4,128)} %param.13) | copy-start | bytes 772
  2.5 23.3 %all-to-all-start = ((bf16[4,64,1280]{2,1,0:T(8,128)(2,1)}), bf16[4,64,1280]{2,1,0:T(8,128)(2,1)S(1)}, u32[]{:S(2)}, u32[]{:S(2)}) async-start(bf16[4,64,1280]{2,1,0:T(8,128)(2,1)} %shard_map.103), calls=%async_computation | async-start | bytes 1310720 | tf_op jit(solution)/shard_map/all_to_all | solution.py:20
  20.6 24.3 %copy-start.1 = (bf16[16,1024]{1,0:T(8,128)(2,1)S(1)}, bf16[16,1024]{1,0:T(8,128)(2,1)}, u32[]{:S(2)}) copy-start(bf16[16,1024]{1,0:T(8,128)(2,1)} %cot_ref.1) | copy-start | bytes 98308
  28.3 39.2 %copy-start = (bf16[1,1024,1024]{2,1,0:T(8,128)(2,1)S(1)}, bf16[1,1024,1024]{2,1,0:T(8,128)(2,1)}, u32[]{:S(2)}) copy-start(bf16[1,1024,1024]{2,1,0:T(8,128)(2,1)} %gate_ref.1) | copy-start | bytes 6291460
  29.1 15.8 %all-to-all-start.1 = ((bf16[8,16,1024]{2,1,0:T(8,128)(2,1)}), bf16[8,16,1024]{2,1,0:T(8,128)(2,1)S(1)}, u32[]{:S(2)}, u32[]{:S(2)}) async-start(bf16[8,16,1024]{2,1,0:T(8,128)(2,1)} %shard_map.105), calls=%async_computation.1 | async-start | bytes 524288 | tf_op jit(solution)/shard_map/all_to_all | solution.py:20

commit v5 on v4

--- a/solution.py
+++ b/solution.py
@@ -70,12 +70,12 @@
     theirs_ref[...] = jnp.where(even, part[:, 1], part[:, 0])
 
 
-def add_body(core_ref, mine_ref, sent_ref, out_ref):
+def add_body(core_ref, mine_ref, sent_ref, _place, _chooser, out_ref):
     other = jnp.where(core_ref[0] == 0, sent_ref[1], sent_ref[0])
     out_ref[...] = (mine_ref[...].astype(f32) + other.astype(f32)).astype(bf16)
 
 
-def dispatch_body(parts_ref, cot_ref, place_ref, _chooser, out_ref):
+def dispatch_body(parts_ref, cot_ref, place_ref, out_ref):
     half = out_ref.shape[1]
     latent = jnp.sum(parts_ref[...].astype(f32), axis=0).astype(bf16)
     cot = cot_ref[...]
@@ -193,12 +193,9 @@
     out_ref[:, block:] = (weight * scale).astype(bf16)
 
 
-def gather_body(parts_ref, grad_x_ref, weight_ref):
-    nx, feats, wide = parts_ref.shape
-    block = grad_x_ref.shape[1] // nx
+def gather_body(parts_ref, weight_ref):
     tiles, tall, half = weight_ref.shape
-    for j in range(nx):
-        grad_x_ref[:, j * block : (j + 1) * block] = parts_ref[j, :, :block]
+    block = parts_ref.shape[2] - 2 * half
     total = jnp.sum(parts_ref[:, :, block:].astype(f32), axis=0).astype(bf16)
     for i in range(tiles):
         a, b = i // 2, i % 2
@@ -210,11 +207,17 @@
     out_ref[...] = jnp.broadcast_to(total[None], out_ref.shape)
 
 
-def finish_body(tiles_ref, out_ref):
+def finish_body(tiles_ref, parts_ref, routed_ref, combined_ref, grad_x_ref, grad_down_ref):
+    nx = parts_ref.shape[0]
+    block = grad_x_ref.shape[1] // nx
     tiles, tall, half = tiles_ref.shape
+    combined_ref[...] = routed_ref[...]
+    for j in range(nx):
+        grad_x_ref[:, j * block : (j + 1) * block] = parts_ref[j, :, :block]
     for i in range(tiles):
         a, b = i // 2, i % 2
-        out_ref[a * tall : (a + 1) * tall, b * half : (b + 1) * half] = tiles_ref[i].astype(f32)
+        rows, lanes = slice(a * tall, (a + 1) * tall), slice(b * half, (b + 1) * half)
+        grad_down_ref[rows, lanes] = tiles_ref[i].astype(f32)
 
 
 def on_device(x_t, down_proj, w_gate, w_value, w_out, routes, gate_fix, cotangent):
@@ -252,10 +255,6 @@
         specs=[smem, vmem],
     )
     sent = lax.all_gather(theirs, "c", axis=0, tiled=False)
-    partial = local(
-        add_body, shape(ny, tok_dev, width), core, mine, sent, specs=[smem, vmem, vmem]
-    )
-    parts = swap(partial, "y")
 
     flat = routes.reshape(-1)
     chosen = (flat[:, None] == jnp.arange(groups, dtype=jnp.int32)[None, :]).astype(bf16)
@@ -291,14 +290,23 @@
         axis=0,
     ).astype(bf16)
 
+    partial = local(
+        add_body,
+        shape(ny, tok_dev, width),
+        core,
+        mine,
+        sent,
+        where,
+        chooser,
+        specs=[smem, vmem, vmem, anywhere, anywhere],
+    )
+    parts = swap(partial, "y")
     send = local(
         dispatch_body,
         shape(groups * 8, half),
         parts,
         cotangent,
         where,
-        chooser,
-        specs=[vmem, vmem, vmem, anywhere],
     )
     got = swap(send.reshape(groups, 8, half), ("x", "y", "c")).reshape(groups * 8, half)
     reply = local(
@@ -317,7 +325,7 @@
         limit=50,
     )
     back = swap(reply.reshape(groups, 8, half), ("x", "y", "c")).reshape(groups * 8, half)
-    combined, by_owner = local(
+    routed, by_owner = local(
         combine_body, (shape(tok_dev, width), shape(ny, tok_dev, width)), back, chooser
     )
 
@@ -331,16 +339,19 @@
         scale=1.0 / math.sqrt(tokens * nz),
     )
     packed_back = swap(packed_back.reshape(nx, feats, block + width), "x")
-    grad_x, weight_tiles = local(
-        gather_body, (shape(feats, tokens), shape(16, feats // 8, half)), packed_back
-    )
+    weight_tiles = local(gather_body, shape(16, feats // 8, half), packed_back)
 
     tall = 16 // nz * feats // 8
     own = swap(weight_tiles.reshape(nz, tall, half), "dp")
     own = local(sum_body, shape(nz, tall, half), own)
     tiles = swap(own, "dp").reshape(16, feats // 8, half)
-    grad_down = local(finish_body, shape(feats, width, dtype=f32), tiles)
-    return (combined, grad_x, grad_down)
+    return local(
+        finish_body,
+        (shape(tok_dev, width), shape(feats, tokens), shape(feats, width, dtype=f32)),
+        tiles,
+        packed_back,
+        routed,
+    )
 
 
 def solution(mesh):

time: 174 us -> 172 us (0.989)
  blocking collectives: 122 us -> 138 us
  waiting for transfers between devices: 17.2 us -> 4.84 us
  starting transfers between devices: 20 us -> 16.6 us
  Pallas kernels: 11.1 us -> 9.2 us
    all_to_all x6 -> x7, blocking collectives: 118 us -> 133 us  [swap(): return lax.all_to_all(blocks, axes, split_axis=0, concat_axis=0, tiled=True)]
    all_to_all x2 -> x1, waiting for transfers between devices: 17.2 us -> 4.84 us  [swap(): return lax.all_to_all(blocks, axes, split_axis=0, concat_axis=0, tiled=True)]
    all_to_all x2 -> x1, starting transfers between devices: 20 us -> 16.6 us  [swap(): return lax.all_to_all(blocks, axes, split_axis=0, concat_axis=0, tiled=True)]
    pallas_call x10, Pallas kernels: 11.1 us -> 9.2 us  [local(): pl.pallas_call(functools.partial(body, **static) if static else body, out...]
  transfers between devices with their start and end apart: 2 -> 1, of which waited for: 2 -> 1; matrix products, arithmetic and copies ran while one was open for 1% -> 1% of each run, Pallas kernels for 0% -> 0%
where the time goes in v5:
time: 172 us; the launch traced here: 171 us
  blocking collectives  138 us (80%)
  starting transfers between devices  16.6 us (10%)
  Pallas kernels  9.2 us (5%)
  waiting for transfers between devices  4.84 us (3%)
    all_to_all x7, blocking collectives, swap(): return lax.all_to_all(blocks, axes, split_axis=0, concat_axis=0, tiled=True)  133 us
    all_to_all x1, starting transfers between devices, swap(): return lax.all_to_all(blocks, axes, split_axis=0, concat_axis=0, tiled=True)  16.6 us
    pallas_call x10, Pallas kernels, local(): pl.pallas_call(functools.partial(body, **static) if static else body, out...  9.2 us
    all_to_all x1, waiting for transfers between devices, swap(): return lax.all_to_all(blocks, axes, split_axis=0, concat_axis=0, tiled=True)  4.84 us
  transfers between devices with their start and end apart: 1, of which 1 were waited for; matrix products, arithmetic and copies ran while one was open for 1% of the time, Pallas kernels for 0%

profile of v5, /device:TPU:6, one launch (start us, length us, event | category | flops | bytes accessed | tf_op | source)
XLA Modules:
  0.0 171.0 jit_solution(16602599173410959477)
XLA Ops:
  0.6 0.0 copy-start.3
  0.6 0.0 copy-start.2
  0.7 1.9 %shard_map.103 = bf16[4,64,1280]{2,1,0:T(8,128)(2,1)} custom-call(bf16[64,1024]{1,0:T(8,128)(2,1)} %x_hbm.1, bf16[64,1024]{1,0:T(8,128)(2,1)} %proj_hbm.1), custom_call_target="tpu_custom_call" | custom-call | tf_op jit(solution)/shard_map/pallas_call | solution.py:30
  2.5 16.6 %all-to-all-start = ((bf16[4,64,1280]{2,1,0:T(8,128)(2,1)}), bf16[4,64,1280]{2,1,0:T(8,128)(2,1)S(1)}, u32[]{:S(2)}, u32[]{:S(2)}) async-start(bf16[4,64,1280]{2,1,0:T(8,128)(2,1)} %shard_map.103), calls=%async_computation | async-start | bytes 1310720 | tf_op jit(solution)/shard_map/all_to_all | solution.py:20
  19.2 0.0 copy-done.3
  19.3 0.0 copy-done.2
  19.3 0.1 copy.38
  19.4 0.1 eq.164
  19.5 0.2 fusion
  19.6 0.1 convert_element_type.30
  19.7 0.1 copy.39
  19.8 0.1 fusion.1
  19.9 0.1 copy.42
  20.1 0.1 copy.43
  20.2 0.1 copy.41
  20.3 0.1 copy.40
  20.5 0.1 select_reduce_fusion
  20.6 0.0 copy-start.1
  20.7 0.3 pad_maximum_fusion._place.place_ref
  21.0 4.8 %all-to-all-done = bf16[4,64,1280]{2,1,0:T(8,128)(2,1)S(1)} async-done(((bf16[4,64,1280]{2,1,0:T(8,128)(2,1)}), bf16[4,64,1280]{2,1,0:T(8,128)(2,1)S(1)}, u32[]{:S(2)}, u32[]{:S(2)}) %all-to-all-start) | async-done | bytes 655392 | tf_op jit(solution)/shard_map/all_to_all | solution.py:20
  25.8 0.3 shard_map.104
  26.2 2.2 %all-gather = bf16[16,16,1024]{2,1,0:T(8,128)(2,1)S(1)} all-gather(bf16[8,16,1024]{2,1,0:T(8,128)(2,1)S(1)} %get-tuple-element.8), channel_id=2, replica_groups=mesh['x'=4,'y'=8,'c'=2,'dp'=16] {'c'}, dimensions={0}, use_global_device_ids=true | all-gather | bytes 786432 | tf_op jit(solution)/shard_map/all_gather | solution.py:257
  28.3 0.0 copy-start
  28.3 0.1 shard_map.105
  28.4 15.0 %all_to_all.40.parts_ref = bf16[8,16,1024]{2,1,0:T(8,128)(2,1)S(1)} all-to-all(bf16[8,16,1024]{2,1,0:T(8,128)(2,1)S(1)} %shard_map.105), channel_id=1, replica_groups=mesh['x'=4,'y'=8,'c'=2,'dp'=16] {'y'}, dimensions={0} | all-to-all | bytes 524288 | tf_op jit(solution)/shard_map/all_to_all | solution.py:20
  43.4 0.0 copy-done.1
  43.4 0.3 shard_map.106
  43.7 22.3 %all_to_all.41 = bf16[64,8,512]{2,1,0:T(8,128)(2,1)S(1)} all-to-all(bf16[64,8,512]{2,1,0:T(8,128)(2,1)S(1)} %bitcast.17), channel_id=1, replica_groups=mesh['x'=4,'y'=8,'c'=2,'dp'=16] {'x','y','c'}, dimensions={0} | all-to-all | bytes 1048576 | tf_op jit(solution)/shard_map/all_to_all | solution.py:20
  66.1 0.0 copy-done
  66.1 5.1 %shard_map.107 = bf16[512,512]{1,0:T(8,128)(2,1)S(1)} custom-call(bf16[512,512]{1,0:T(8,128)(2,1)S(1)} %bitcast.12, bf16[1,1024,1024]{2,1,0:T(8,128)(2,1)S(1)} %copy-done, bf16[1,1024,1024]{2,1,0:T(8,128)(2,1)} %value_hbm.1, bf16[1,1024,1024]{2,1,0:T(8,128)(2,1)} %outw_hbm.1), custom_call_target="tpu_custom_call" | custom-call | tf_op jit(solution)/shard_map/pallas_call | solution.py:30
  71.2 23.4 %all_to_all.42 = bf16[64,8,512]{2,1,0:T(8,128)(2,1)S(1)} all-to-all(bf16[64,8,512]{2,1,0:T(8,128)(2,1)S(1)} %bitcast.13), channel_id=1, replica_groups=mesh['x'=4,'y'=8,'c'=2,'dp'=16] {'x','y','c'}, dimensions={0} | all-to-all | bytes 1048576 | tf_op jit(solution)/shard_map/all_to_all | solution.py:20
  94.6 0.2 shard_map.108
  94.8 15.3 %all_to_all.43 = bf16[8,16,1024]{2,1,0:T(8,128)(2,1)S(1)} all-to-all(bf16[8,16,1024]{2,1,0:T(8,128)(2,1)S(1)} %get-tuple-element.9), channel_id=1, replica_groups=mesh['x'=4,'y'=8,'c'=2,'dp'=16] {'y'}, dimensions={0} | all-to-all | bytes 524288 | tf_op jit(solution)/shard_map/all_to_all | solution.py:20
  110.1 2.2 %all-gather.1 = bf16[16,16,1024]{2,1,0:T(8,128)(2,1)S(1)} all-gather(bf16[8,16,1024]{2,1,0:T(8,128)(2,1)S(1)} %all_to_all.43), channel_id=3, replica_groups=mesh['x'=4,'y'=8,'c'=2,'dp'=16] {'c'}, dimensions={0}, use_global_device_ids=true | all-gather | bytes 786432 | tf_op jit(solution)/shard_map/all_gather | solution.py:333
  112.3 0.5 shard_map.109
  112.8 13.6 %all_to_all.44.parts_ref = bf16[4,64,1280]{2,1,0:T(8,128)(2,1)S(1)} all-to-all(bf16[4,64,1280]{2,1,0:T(8,128)(2,1)S(1)} %bitcast.11), channel_id=1, replica_groups=mesh['x'=4,'y'=8,'c'=2,'dp'=16] {'x'}, dimensions={0} | all-to-all | bytes 1310720 | tf_op jit(solution)/shard_map/all_to_all | solution.py:20
  126.4 0.1 shard_map.110
  126.5 27.2 %all_to_all.45.parts_ref = bf16[16,8,512]{2,1,0:T(8,128)(2,1)S(1)} all-to-all(bf16[16,8,512]{2,1,0:T(8,128)(2,1)S(1)} %shard_map.110), channel_id=1, replica_groups=mesh['x'=4,'y'=8,'c'=2,'dp'=16] {'dp'}, dimensions={0} | all-to-all | bytes 262144 | tf_op jit(solution)/shard_map/all_to_all | solution.py:20
  153.6 16.6 %all_to_all.46.tiles_ref = bf16[16,8,512]{2,1,0:T(8,128)(2,1)S(1)} all-to-all(bf16[16,8,512]{2,1,0:T(8,128)(2,1)S(1)} %shard_map.111), channel_id=1, replica_groups=mesh['x'=4,'y'=8,'c'=2,'dp'=16] {'dp'}, dimensions={0} | all-to-all | bytes 262144 | tf_op jit(solution)/shard_map/all_to_all | solution.py:20
  170.2 0.8 shard_map.112
  (21 shorter events, 0.2 us)
Async XLA Ops:
  0.6 18.6 %copy-start.3 = (s32[16,4]{0,1:T(4,128)S(1)}, s32[16,4]{0,1:T(4,128)}, u32[]{:S(2)}) copy-start(s32[16,4]{0,1:T(4,128)} %param.14) | copy-start | bytes 772
  0.6 18.6 %copy-start.2 = (s32[16,4]{0,1:T(4,128)S(1)}, s32[16,4]{0,1:T(4,128)}, u32[]{:S(2)}) copy-start(s32[16,4]{0,1:T(4,128)} %param.13) | copy-start | bytes 772
  2.5 23.3 %all-to-all-start = ((bf16[4,64,1280]{2,1,0:T(8,128)(2,1)}), bf16[4,64,1280]{2,1,0:T(8,128)(2,1)S(1)}, u32[]{:S(2)}, u32[]{:S(2)}) async-start(bf16[4,64,1280]{2,1,0:T(8,128)(2,1)} %shard_map.103), calls=%async_computation | async-start | bytes 1310720 | tf_op jit(solution)/shard_map/all_to_all | solution.py:20
  20.6 22.8 %copy-start.1 = (bf16[16,1024]{1,0:T(8,128)(2,1)S(1)}, bf16[16,1024]{1,0:T(8,128)(2,1)}, u32[]{:S(2)}) copy-start(bf16[16,1024]{1,0:T(8,128)(2,1)} %cot_ref.1) | copy-start | bytes 98308
  28.3 37.7 %copy-start = (bf16[1,1024,1024]{2,1,0:T(8,128)(2,1)S(1)}, bf16[1,1024,1024]{2,1,0:T(8,128)(2,1)}, u32[]{:S(2)}) copy-start(bf16[1,1024,1024]{2,1,0:T(8,128)(2,1)} %gate_ref.1) | copy-start | bytes 6291460

commit v6 on v5

--- a/solution.py
+++ b/solution.py
@@ -194,12 +194,13 @@
 
 
 def gather_body(parts_ref, weight_ref):
-    tiles, tall, half = weight_ref.shape
-    block = parts_ref.shape[2] - 2 * half
+    tiles, tall, wide = weight_ref.shape
+    width = wide * 4
+    block = parts_ref.shape[2] - width
     total = jnp.sum(parts_ref[:, :, block:].astype(f32), axis=0).astype(bf16)
     for i in range(tiles):
-        a, b = i // 2, i % 2
-        weight_ref[i] = total[a * tall : (a + 1) * tall, b * half : (b + 1) * half]
+        a, b = i // 4, i % 4
+        weight_ref[i] = total[a * tall : (a + 1) * tall, b * wide : (b + 1) * wide]
 
 
 def sum_body(parts_ref, out_ref):
@@ -210,13 +211,13 @@
 def finish_body(tiles_ref, parts_ref, routed_ref, combined_ref, grad_x_ref, grad_down_ref):
     nx = parts_ref.shape[0]
     block = grad_x_ref.shape[1] // nx
-    tiles, tall, half = tiles_ref.shape
+    tiles, tall, wide = tiles_ref.shape
     combined_ref[...] = routed_ref[...]
     for j in range(nx):
         grad_x_ref[:, j * block : (j + 1) * block] = parts_ref[j, :, :block]
     for i in range(tiles):
-        a, b = i // 2, i % 2
-        rows, lanes = slice(a * tall, (a + 1) * tall), slice(b * half, (b + 1) * half)
+        a, b = i // 4, i % 4
+        rows, lanes = slice(a * tall, (a + 1) * tall), slice(b * wide, (b + 1) * wide)
         grad_down_ref[rows, lanes] = tiles_ref[i].astype(f32)
 
 
@@ -339,12 +340,12 @@
         scale=1.0 / math.sqrt(tokens * nz),
     )
     packed_back = swap(packed_back.reshape(nx, feats, block + width), "x")
-    weight_tiles = local(gather_body, shape(16, feats // 8, half), packed_back)
-
-    tall = 16 // nz * feats // 8
-    own = swap(weight_tiles.reshape(nz, tall, half), "dp")
-    own = local(sum_body, shape(nz, tall, half), own)
-    tiles = swap(own, "dp").reshape(16, feats // 8, half)
+    weight_tiles = local(gather_body, shape(16, feats // 4, width // 4), packed_back)
+
+    tall = 16 // nz * feats // 4
+    own = swap(weight_tiles.reshape(nz, tall, width // 4), "dp")
+    own = local(sum_body, shape(nz, tall, width // 4), own)
+    tiles = swap(own, "dp").reshape(16, feats // 4, width // 4)
     return local(
         finish_body,
         (shape(tok_dev, width), shape(feats, tokens), shape(feats, width, dtype=f32)),

time: 172 us -> 172 us (level)
  no operation moved by 1% of the time
where the time goes in v6:
time: 172 us; the launch traced here: 171 us
  blocking collectives  138 us (80%)
  starting transfers between devices  16.6 us (10%)
  Pallas kernels  9.2 us (5%)
  waiting for transfers between devices  4.84 us (3%)
    all_to_all x7, blocking collectives, swap(): return lax.all_to_all(blocks, axes, split_axis=0, concat_axis=0, tiled=True)  133 us
    all_to_all x1, starting transfers between devices, swap(): return lax.all_to_all(blocks, axes, split_axis=0, concat_axis=0, tiled=True)  16.6 us
    pallas_call x10, Pallas kernels, local(): pl.pallas_call(functools.partial(body, **static) if static else body, out...  9.2 us
    all_to_all x1, waiting for transfers between devices, swap(): return lax.all_to_all(blocks, axes, split_axis=0, concat_axis=0, tiled=True)  4.84 us
  transfers between devices with their start and end apart: 1, of which 1 were waited for; matrix products, arithmetic and copies ran while one was open for 1% of the time, Pallas kernels for 0%

profile of v6, /device:TPU:6, one launch (start us, length us, event | category | flops | bytes accessed | tf_op | source)
XLA Modules:
  0.0 171.0 jit_solution(5520431820492421112)
XLA Ops:
  0.6 0.0 copy-start.3
  0.6 0.0 copy-start.2
  0.7 1.9 %shard_map.103 = bf16[4,64,1280]{2,1,0:T(8,128)(2,1)} custom-call(bf16[64,1024]{1,0:T(8,128)(2,1)} %x_hbm.1, bf16[64,1024]{1,0:T(8,128)(2,1)} %proj_hbm.1), custom_call_target="tpu_custom_call" | custom-call | tf_op jit(solution)/shard_map/pallas_call | solution.py:30
  2.5 16.6 %all-to-all-start = ((bf16[4,64,1280]{2,1,0:T(8,128)(2,1)}), bf16[4,64,1280]{2,1,0:T(8,128)(2,1)S(1)}, u32[]{:S(2)}, u32[]{:S(2)}) async-start(bf16[4,64,1280]{2,1,0:T(8,128)(2,1)} %shard_map.103), calls=%async_computation | async-start | bytes 1310720 | tf_op jit(solution)/shard_map/all_to_all | solution.py:20
  19.2 0.0 copy-done.3
  19.3 0.0 copy-done.2
  19.3 0.1 copy.38
  19.4 0.1 eq.164
  19.5 0.2 fusion
  19.6 0.1 convert_element_type.30
  19.7 0.1 copy.39
  19.8 0.1 fusion.1
  19.9 0.1 copy.42
  20.1 0.1 copy.43
  20.2 0.1 copy.41
  20.3 0.1 copy.40
  20.5 0.1 select_reduce_fusion
  20.6 0.0 copy-start.1
  20.7 0.3 pad_maximum_fusion._place.place_ref
  21.0 4.8 %all-to-all-done = bf16[4,64,1280]{2,1,0:T(8,128)(2,1)S(1)} async-done(((bf16[4,64,1280]{2,1,0:T(8,128)(2,1)}), bf16[4,64,1280]{2,1,0:T(8,128)(2,1)S(1)}, u32[]{:S(2)}, u32[]{:S(2)}) %all-to-all-start) | async-done | bytes 655392 | tf_op jit(solution)/shard_map/all_to_all | solution.py:20
  25.8 0.3 shard_map.104
  26.2 2.2 %all-gather = bf16[16,16,1024]{2,1,0:T(8,128)(2,1)S(1)} all-gather(bf16[8,16,1024]{2,1,0:T(8,128)(2,1)S(1)} %get-tuple-element.8), channel_id=2, replica_groups=mesh['x'=4,'y'=8,'c'=2,'dp'=16] {'c'}, dimensions={0}, use_global_device_ids=true | all-gather | bytes 786432 | tf_op jit(solution)/shard_map/all_gather | solution.py:258
  28.3 0.0 copy-start
  28.3 0.1 shard_map.105
  28.4 15.0 %all_to_all.40.parts_ref = bf16[8,16,1024]{2,1,0:T(8,128)(2,1)S(1)} all-to-all(bf16[8,16,1024]{2,1,0:T(8,128)(2,1)S(1)} %shard_map.105), channel_id=1, replica_groups=mesh['x'=4,'y'=8,'c'=2,'dp'=16] {'y'}, dimensions={0} | all-to-all | bytes 524288 | tf_op jit(solution)/shard_map/all_to_all | solution.py:20
  43.4 0.0 copy-done.1
  43.4 0.3 shard_map.106
  43.7 22.3 %all_to_all.41 = bf16[64,8,512]{2,1,0:T(8,128)(2,1)S(1)} all-to-all(bf16[64,8,512]{2,1,0:T(8,128)(2,1)S(1)} %bitcast.17), channel_id=1, replica_groups=mesh['x'=4,'y'=8,'c'=2,'dp'=16] {'x','y','c'}, dimensions={0} | all-to-all | bytes 1048576 | tf_op jit(solution)/shard_map/all_to_all | solution.py:20
  66.1 0.0 copy-done
  66.1 5.1 %shard_map.107 = bf16[512,512]{1,0:T(8,128)(2,1)S(1)} custom-call(bf16[512,512]{1,0:T(8,128)(2,1)S(1)} %bitcast.12, bf16[1,1024,1024]{2,1,0:T(8,128)(2,1)S(1)} %copy-done, bf16[1,1024,1024]{2,1,0:T(8,128)(2,1)} %value_hbm.1, bf16[1,1024,1024]{2,1,0:T(8,128)(2,1)} %outw_hbm.1), custom_call_target="tpu_custom_call" | custom-call | tf_op jit(solution)/shard_map/pallas_call | solution.py:30
  71.2 23.4 %all_to_all.42 = bf16[64,8,512]{2,1,0:T(8,128)(2,1)S(1)} all-to-all(bf16[64,8,512]{2,1,0:T(8,128)(2,1)S(1)} %bitcast.13), channel_id=1, replica_groups=mesh['x'=4,'y'=8,'c'=2,'dp'=16] {'x','y','c'}, dimensions={0} | all-to-all | bytes 1048576 | tf_op jit(solution)/shard_map/all_to_all | solution.py:20
  94.6 0.2 shard_map.108
  94.8 15.3 %all_to_all.43 = bf16[8,16,1024]{2,1,0:T(8,128)(2,1)S(1)} all-to-all(bf16[8,16,1024]{2,1,0:T(8,128)(2,1)S(1)} %get-tuple-element.9), channel_id=1, replica_groups=mesh['x'=4,'y'=8,'c'=2,'dp'=16] {'y'}, dimensions={0} | all-to-all | bytes 524288 | tf_op jit(solution)/shard_map/all_to_all | solution.py:20
  110.1 2.2 %all-gather.1 = bf16[16,16,1024]{2,1,0:T(8,128)(2,1)S(1)} all-gather(bf16[8,16,1024]{2,1,0:T(8,128)(2,1)S(1)} %all_to_all.43), channel_id=3, replica_groups=mesh['x'=4,'y'=8,'c'=2,'dp'=16] {'c'}, dimensions={0}, use_global_device_ids=true | all-gather | bytes 786432 | tf_op jit(solution)/shard_map/all_gather | solution.py:334
  112.3 0.5 shard_map.109
  112.8 13.6 %all_to_all.44.parts_ref = bf16[4,64,1280]{2,1,0:T(8,128)(2,1)S(1)} all-to-all(bf16[4,64,1280]{2,1,0:T(8,128)(2,1)S(1)} %bitcast.11), channel_id=1, replica_groups=mesh['x'=4,'y'=8,'c'=2,'dp'=16] {'x'}, dimensions={0} | all-to-all | bytes 1310720 | tf_op jit(solution)/shard_map/all_to_all | solution.py:20
  126.4 0.1 shard_map.110
  126.5 27.2 %all_to_all.45.parts_ref = bf16[16,16,256]{2,1,0:T(8,128)(2,1)S(1)} all-to-all(bf16[16,16,256]{2,1,0:T(8,128)(2,1)S(1)} %shard_map.110), channel_id=1, replica_groups=mesh['x'=4,'y'=8,'c'=2,'dp'=16] {'dp'}, dimensions={0} | all-to-all | bytes 262144 | tf_op jit(solution)/shard_map/all_to_all | solution.py:20
  153.6 16.6 %all_to_all.46.tiles_ref = bf16[16,16,256]{2,1,0:T(8,128)(2,1)S(1)} all-to-all(bf16[16,16,256]{2,1,0:T(8,128)(2,1)S(1)} %shard_map.111), channel_id=1, replica_groups=mesh['x'=4,'y'=8,'c'=2,'dp'=16] {'dp'}, dimensions={0} | all-to-all | bytes 262144 | tf_op jit(solution)/shard_map/all_to_all | solution.py:20
  170.2 0.8 shard_map.112
  (21 shorter events, 0.2 us)
Async XLA Ops:
  0.6 18.6 %copy-start.3 = (s32[16,4]{0,1:T(4,128)S(1)}, s32[16,4]{0,1:T(4,128)}, u32[]{:S(2)}) copy-start(s32[16,4]{0,1:T(4,128)} %param.14) | copy-start | bytes 772
  0.6 18.6 %copy-start.2 = (s32[16,4]{0,1:T(4,128)S(1)}, s32[16,4]{0,1:T(4,128)}, u32[]{:S(2)}) copy-start(s32[16,4]{0,1:T(4,128)} %param.13) | copy-start | bytes 772
  2.5 23.3 %all-to-all-start = ((bf16[4,64,1280]{2,1,0:T(8,128)(2,1)}), bf16[4,64,1280]{2,1,0:T(8,128)(2,1)S(1)}, u32[]{:S(2)}, u32[]{:S(2)}) async-start(bf16[4,64,1280]{2,1,0:T(8,128)(2,1)} %shard_map.103), calls=%async_computation | async-start | bytes 1310720 | tf_op jit(solution)/shard_map/all_to_all | solution.py:20
  20.6 22.8 %copy-start.1 = (bf16[16,1024]{1,0:T(8,128)(2,1)S(1)}, bf16[16,1024]{1,0:T(8,128)(2,1)}, u32[]{:S(2)}) copy-start(bf16[16,1024]{1,0:T(8,128)(2,1)} %cot_ref.1) | copy-start | bytes 98308
  28.3 37.7 %copy-start = (bf16[1,1024,1024]{2,1,0:T(8,128)(2,1)S(1)}, bf16[1,1024,1024]{2,1,0:T(8,128)(2,1)}, u32[]{:S(2)}) copy-start(bf16[1,1024,1024]{2,1,0:T(8,128)(2,1)} %gate_ref.1) | copy-start | bytes 6291460

commit v7 on v6

--- a/solution.py
+++ b/solution.py
@@ -223,7 +223,8 @@
 
 def on_device(x_t, down_proj, w_gate, w_value, w_out, routes, gate_fix, cotangent):
     nx, ny, nc = lax.axis_size("x"), lax.axis_size("y"), lax.axis_size("c")
-    nz = lax.axis_size("dp")
+    far, near = lax.axis_size("zh"), lax.axis_size("zl")
+    nz = far * near
     groups = nx * ny * nc
     feats, width = down_proj.shape
     half = width // 2
@@ -342,10 +343,11 @@
     packed_back = swap(packed_back.reshape(nx, feats, block + width), "x")
     weight_tiles = local(gather_body, shape(16, feats // 4, width // 4), packed_back)
 
-    tall = 16 // nz * feats // 4
-    own = swap(weight_tiles.reshape(nz, tall, width // 4), "dp")
-    own = local(sum_body, shape(nz, tall, width // 4), own)
-    tiles = swap(own, "dp").reshape(16, feats // 4, width // 4)
+    tall = 16 // near * feats // 4
+    own = swap(weight_tiles.reshape(near, tall, width // 4), "zl")
+    own = local(sum_body, shape(far, tall, width // 4), own)
+    own = local(sum_body, shape(near, tall, width // 4), swap(own, "zh"))
+    tiles = swap(own, "zl").reshape(16, feats // 4, width // 4)
     return local(
         finish_body,
         (shape(tok_dev, width), shape(feats, tokens), shape(feats, width, dtype=f32)),
@@ -360,11 +362,15 @@
     core = 2
     ny = 8
     nx = mesh.shape["expert"] // (ny * core)
-    fine = Mesh(mesh.devices.reshape(nx, ny, core, dp), ("x", "y", "c", "dp"))
+    near = 4
+    fine = Mesh(
+        mesh.devices.reshape(nx, ny, core, dp // near, near), ("x", "y", "c", "zh", "zl")
+    )
+    batch = ("zh", "zl")
     expert = ("x", "y", "c")
-    tokens = ("dp", "x", "y", "c")
+    tokens = ("zh", "zl", "x", "y", "c")
     placed = (
-        P(expert, "dp"),
+        P(expert, batch),
         P(expert, None),
         P(expert, None, None),
         P(expert, None, None),
@@ -377,6 +383,6 @@
         on_device,
         mesh=fine,
         in_specs=placed,
-        out_specs=(P(tokens, None), P(expert, "dp"), P(expert, None)),
+        out_specs=(P(tokens, None), P(expert, batch), P(expert, None)),
         check_vma=False,
     )

time: 172 us -> 175 us (1.017)
  blocking collectives: 138 us -> 140 us
    all_to_all x7 -> x8, blocking collectives: 133 us -> 136 us  [swap(): return lax.all_to_all(blocks, axes, split_axis=0, concat_axis=0, tiled=True)]
    pallas_call x10 -> x11, Pallas kernels: 9.2 us -> 9.22 us  [local(): pl.pallas_call(functools.partial(body, **static) if static else body, out...]
where the time goes in v7:
time: 175 us; the launch traced here: 174 us
  blocking collectives  140 us (80%)
  starting transfers between devices  16.6 us (9%)
  Pallas kernels  9.22 us (5%)
  waiting for transfers between devices  4.84 us (3%)
    all_to_all x8, blocking collectives, swap(): return lax.all_to_all(blocks, axes, split_axis=0, concat_axis=0, tiled=True)  136 us
    all_to_all x1, starting transfers between devices, swap(): return lax.all_to_all(blocks, axes, split_axis=0, concat_axis=0, tiled=True)  16.6 us
    pallas_call x11, Pallas kernels, local(): pl.pallas_call(functools.partial(body, **static) if static else body, out...  9.22 us
    all_to_all x1, waiting for transfers between devices, swap(): return lax.all_to_all(blocks, axes, split_axis=0, concat_axis=0, tiled=True)  4.84 us
  transfers between devices with their start and end apart: 1, of which 1 were waited for; matrix products, arithmetic and copies ran while one was open for 1% of the time, Pallas kernels for 0%

profile of v7, /device:TPU:6, one launch (start us, length us, event | category | flops | bytes accessed | tf_op | source)
XLA Modules:
  0.0 173.6 jit_solution(34193480390032120)
XLA Ops:
  0.6 0.0 copy-start.3
  0.6 0.0 copy-start.2
  0.7 1.9 %shard_map.103 = bf16[4,64,1280]{2,1,0:T(8,128)(2,1)} custom-call(bf16[64,1024]{1,0:T(8,128)(2,1)} %x_hbm.1, bf16[64,1024]{1,0:T(8,128)(2,1)} %proj_hbm.1), custom_call_target="tpu_custom_call" | custom-call | tf_op jit(solution)/shard_map/pallas_call | solution.py:30
  2.5 16.6 %all-to-all-start = ((bf16[4,64,1280]{2,1,0:T(8,128)(2,1)}), bf16[4,64,1280]{2,1,0:T(8,128)(2,1)S(1)}, u32[]{:S(2)}, u32[]{:S(2)}) async-start(bf16[4,64,1280]{2,1,0:T(8,128)(2,1)} %shard_map.103), calls=%async_computation | async-start | bytes 1310720 | tf_op jit(solution)/shard_map/all_to_all | solution.py:20
  19.2 0.0 copy-done.3
  19.3 0.0 copy-done.2
  19.3 0.1 copy.38
  19.4 0.1 eq.164
  19.5 0.2 fusion
  19.6 0.1 convert_element_type.30
  19.7 0.1 copy.39
  19.8 0.1 fusion.1
  19.9 0.1 copy.42
  20.1 0.1 copy.43
  20.2 0.1 copy.41
  20.3 0.1 copy.40
  20.5 0.1 select_reduce_fusion
  20.6 0.0 copy-start.1
  20.7 0.3 pad_maximum_fusion._place.place_ref
  21.0 4.8 %all-to-all-done = bf16[4,64,1280]{2,1,0:T(8,128)(2,1)S(1)} async-done(((bf16[4,64,1280]{2,1,0:T(8,128)(2,1)}), bf16[4,64,1280]{2,1,0:T(8,128)(2,1)S(1)}, u32[]{:S(2)}, u32[]{:S(2)}) %all-to-all-start) | async-done | bytes 655392 | tf_op jit(solution)/shard_map/all_to_all | solution.py:20
  25.8 0.3 shard_map.104
  26.2 2.2 %all-gather = bf16[16,16,1024]{2,1,0:T(8,128)(2,1)S(1)} all-gather(bf16[8,16,1024]{2,1,0:T(8,128)(2,1)S(1)} %get-tuple-element.8), channel_id=2, replica_groups=mesh['x'=4,'y'=8,'c'=2,'zh'=4,'zl'=4] {'c'}, dimensions={0}, use_global_device_ids=true | all-gather | bytes 786432 | tf_op jit(solution)/shard_map/all_gather | solution.py:259
  28.3 0.0 copy-start
  28.3 0.1 shard_map.105
  28.4 15.0 %all_to_all.45.parts_ref = bf16[8,16,1024]{2,1,0:T(8,128)(2,1)S(1)} all-to-all(bf16[8,16,1024]{2,1,0:T(8,128)(2,1)S(1)} %shard_map.105), channel_id=1, replica_groups=mesh['x'=4,'y'=8,'c'=2,'zh'=4,'zl'=4] {'y'}, dimensions={0} | all-to-all | bytes 524288 | tf_op jit(solution)/shard_map/all_to_all | solution.py:20
  43.4 0.0 copy-done.1
  43.4 0.3 shard_map.106
  43.7 22.3 %all_to_all.46 = bf16[64,8,512]{2,1,0:T(8,128)(2,1)S(1)} all-to-all(bf16[64,8,512]{2,1,0:T(8,128)(2,1)S(1)} %bitcast.19), channel_id=1, replica_groups=mesh['x'=4,'y'=8,'c'=2,'zh'=4,'zl'=4] {'x','y','c'}, dimensions={0} | all-to-all | bytes 1048576 | tf_op jit(solution)/shard_map/all_to_all | solution.py:20
  66.1 0.0 copy-done
  66.1 5.1 %shard_map.107 = bf16[512,512]{1,0:T(8,128)(2,1)S(1)} custom-call(bf16[512,512]{1,0:T(8,128)(2,1)S(1)} %bitcast.14, bf16[1,1024,1024]{2,1,0:T(8,128)(2,1)S(1)} %copy-done, bf16[1,1024,1024]{2,1,0:T(8,128)(2,1)} %value_hbm.1, bf16[1,1024,1024]{2,1,0:T(8,128)(2,1)} %outw_hbm.1), custom_call_target="tpu_custom_call" | custom-call | tf_op jit(solution)/shard_map/pallas_call | solution.py:30
  71.2 23.4 %all_to_all.47 = bf16[64,8,512]{2,1,0:T(8,128)(2,1)S(1)} all-to-all(bf16[64,8,512]{2,1,0:T(8,128)(2,1)S(1)} %bitcast.15), channel_id=1, replica_groups=mesh['x'=4,'y'=8,'c'=2,'zh'=4,'zl'=4] {'x','y','c'}, dimensions={0} | all-to-all | bytes 1048576 | tf_op jit(solution)/shard_map/all_to_all | solution.py:20
  94.6 0.2 shard_map.108
  94.8 15.3 %all_to_all.48 = bf16[8,16,1024]{2,1,0:T(8,128)(2,1)S(1)} all-to-all(bf16[8,16,1024]{2,1,0:T(8,128)(2,1)S(1)} %get-tuple-element.9), channel_id=1, replica_groups=mesh['x'=4,'y'=8,'c'=2,'zh'=4,'zl'=4] {'y'}, dimensions={0} | all-to-all | bytes 524288 | tf_op jit(solution)/shard_map/all_to_all | solution.py:20
  110.1 2.2 %all-gather.1 = bf16[16,16,1024]{2,1,0:T(8,128)(2,1)S(1)} all-gather(bf16[8,16,1024]{2,1,0:T(8,128)(2,1)S(1)} %all_to_all.48), channel_id=3, replica_groups=mesh['x'=4,'y'=8,'c'=2,'zh'=4,'zl'=4] {'c'}, dimensions={0}, use_global_device_ids=true | all-gather | bytes 786432 | tf_op jit(solution)/shard_map/all_gather | solution.py:335
  112.3 0.5 shard_map.109
  112.8 13.6 %all_to_all.49.parts_ref = bf16[4,64,1280]{2,1,0:T(8,128)(2,1)S(1)} all-to-all(bf16[4,64,1280]{2,1,0:T(8,128)(2,1)S(1)} %bitcast.13), channel_id=1, replica_groups=mesh['x'=4,'y'=8,'c'=2,'zh'=4,'zl'=4] {'x'}, dimensions={0} | all-to-all | bytes 1310720 | tf_op jit(solution)/shard_map/all_to_all | solution.py:20
  126.4 0.1 shard_map.110
  126.5 8.3 %all_to_all.50.parts_ref = bf16[4,64,256]{2,1,0:T(8,128)(2,1)S(1)} all-to-all(bf16[4,64,256]{2,1,0:T(8,128)(2,1)S(1)} %bitcast.21), channel_id=1, replica_groups=mesh['x'=4,'y'=8,'c'=2,'zh'=4,'zl'=4] {'zl'}, dimensions={0} | all-to-all | bytes 262144 | tf_op jit(solution)/shard_map/all_to_all | solution.py:20
  134.8 28.3 %all_to_all.51.parts_ref = bf16[4,64,256]{2,1,0:T(8,128)(2,1)S(1)} all-to-all(bf16[4,64,256]{2,1,0:T(8,128)(2,1)S(1)} %shard_map.111), channel_id=1, replica_groups=mesh['x'=4,'y'=8,'c'=2,'zh'=4,'zl'=4] {'zh'}, dimensions={0} | all-to-all | bytes 262144 | tf_op jit(solution)/shard_map/all_to_all | solution.py:20
  163.2 9.7 %all_to_all.52 = bf16[4,64,256]{2,1,0:T(8,128)(2,1)S(1)} all-to-all(bf16[4,64,256]{2,1,0:T(8,128)(2,1)S(1)} %shard_map.112), channel_id=1, replica_groups=mesh['x'=4,'y'=8,'c'=2,'zh'=4,'zl'=4] {'zl'}, dimensions={0} | all-to-all | bytes 262144 | tf_op jit(solution)/shard_map/all_to_all | solution.py:20
  172.8 0.8 shard_map.113
  (22 shorter events, 0.2 us)
Async XLA Ops:
  0.6 18.6 %copy-start.3 = (s32[16,4]{0,1:T(4,128)S(1)}, s32[16,4]{0,1:T(4,128)}, u32[]{:S(2)}) copy-start(s32[16,4]{0,1:T(4,128)} %param.14) | copy-start | bytes 772
  0.6 18.6 %copy-start.2 = (s32[16,4]{0,1:T(4,128)S(1)}, s32[16,4]{0,1:T(4,128)}, u32[]{:S(2)}) copy-start(s32[16,4]{0,1:T(4,128)} %param.13) | copy-start | bytes 772
  2.5 23.3 %all-to-all-start = ((bf16[4,64,1280]{2,1,0:T(8,128)(2,1)}), bf16[4,64,1280]{2,1,0:T(8,128)(2,1)S(1)}, u32[]{:S(2)}, u32[]{:S(2)}) async-start(bf16[4,64,1280]{2,1,0:T(8,128)(2,1)} %shard_map.103), calls=%async_computation | async-start | bytes 1310720 | tf_op jit(solution)/shard_map/all_to_all | solution.py:20
  20.6 22.8 %copy-start.1 = (bf16[16,1024]{1,0:T(8,128)(2,1)S(1)}, bf16[16,1024]{1,0:T(8,128)(2,1)}, u32[]{:S(2)}) copy-start(bf16[16,1024]{1,0:T(8,128)(2,1)} %cot_ref.1) | copy-start | bytes 98308
  28.3 37.7 %copy-start = (bf16[1,1024,1024]{2,1,0:T(8,128)(2,1)S(1)}, bf16[1,1024,1024]{2,1,0:T(8,128)(2,1)}, u32[]{:S(2)}) copy-start(bf16[1,1024,1024]{2,1,0:T(8,128)(2,1)} %gate_ref.1) | copy-start | bytes 6291460
